TPU v7x, 32 devices: a whole 2x2x4 slice. The times are simulated.
32 devices in a mesh: dp: 8 (over z, x), seq: 4 (over y, core).
Axes of the slice: x: 2, y: 2, z: 4, core: 2. Of those that a mesh axis runs over, the one named last changes fastest.
Arguments:
- inputs: bfloat16 [16, 1024, 768], P('dp', 'seq'), may hold values from -6 to 6
- cotangent: bfloat16 [16, 1024, 768], P('dp', 'seq'), may hold values from -6 to 6
- task_table: int32 [16], P('dp'), may hold values from 0 to 3, as said below
- type_counts: int32 [16, 3], P('dp'), may hold values from 1 to 512, 1024 in all within a row
- gain_one: float32 [2, 768], replicated, may hold values from 0.5 to 1.5
- bias_one: float32 [2, 768], replicated, may hold values from -2 to 2
- proj_qkv: bfloat16 [2, 768, 2304], replicated, may hold values from -0.21875 to 0.21875
- proj_out: bfloat16 [2, 768, 768], replicated, may hold values from -0.875 to 0.875
- gain_two: float32 [2, 768], replicated, may hold values from 0.5 to 1.5
- bias_two: float32 [2, 768], replicated, may hold values from -2 to 2
- proj_up: bfloat16 [2, 768, 3072], replicated, may hold values from -0.21875 to 0.21875
- proj_down: bfloat16 [2, 3072, 768], replicated, may hold values from -0.109375 to 0.109375
Outputs:
- outputs: bfloat16 [16, 1024, 768], P('dp', 'seq')
- back_inputs: float32 [16, 1024, 768], P('dp', 'seq')
- grad_gain_one: float32 [2, 768], P(None, ('dp', 'seq'))
- grad_bias_one: float32 [2, 768], P(None, ('dp', 'seq'))
- grad_qkv: float32 [2, 768, 2304], P(None, ('dp', 'seq'))
- grad_out: float32 [2, 768, 768], P(None, ('dp', 'seq'))
- grad_gain_two: float32 [2, 768], P(None, ('dp', 'seq'))
- grad_bias_two: float32 [2, 768], P(None, ('dp', 'seq'))
- grad_up: float32 [2, 768, 3072], P(None, ('dp', 'seq'))
- grad_down: float32 [2, 3072, 768], P(None, ('dp', 'seq'))
Inputs may be any that keep to these rules, and one draw needn't show every extreme that they name: `task_table`: the first slot of each index of dp holds a task below 3; every task holds at least one sequence; 3 marks an empty slot. `type_counts`: Image, action and text tokens follow one another in that order and fill the sequence.
All inputs are finite; a program needn't handle non-finite values.
Results may differ from a plain program's by a relative error of at most 0.013.
Values may be sent and summed in bfloat16 or wider, within the bound.
A program may use at most 320 MiB of HBM per device.

v0:
```python
import math

import jax
import jax.numpy as jnp
from jax import lax
from jax.sharding import PartitionSpec as P

HEADS = 12
HEAD_DIM = 64
LAYERS = 2
TASKS = 3


epsilon = 1e-05


def norm_rows(rows_in, gain_row, shift_row):
    average = jnp.mean(rows_in, -1, keepdims=True)
    centred = rows_in - average
    spread = jnp.mean(centred * centred, -1, keepdims=True)
    return centred * lax.rsqrt(spread + epsilon) * gain_row + shift_row


def gelu_exact(values_in):
    return jax.nn.gelu(values_in, approximate=False)


def head_scores(queries, key_rows):
    score_scale = 1.0 / math.sqrt(HEAD_DIM)
    return (
        jnp.einsum("schd,sthd->shct", queries, key_rows, preferred_element_type=jnp.float32)
        * score_scale
    )


def layer_forward(stream, weights, allowed):
    gain_a, shift_a, matrix_qkv, matrix_out, gain_b, shift_b, matrix_up, matrix_down = weights
    slots, rows, width = stream.shape
    hidden = norm_rows(stream, gain_a, shift_a).astype(jnp.bfloat16)
    projected = jnp.einsum(
        "scd,de->sce", hidden, matrix_qkv, preferred_element_type=jnp.float32
    ).astype(jnp.bfloat16)
    queries = projected[..., :width].reshape(slots, rows, HEADS, HEAD_DIM)
    local_keys = projected[..., width : 2 * width].reshape(slots, rows, HEADS, HEAD_DIM)
    local_values = projected[..., 2 * width :].reshape(slots, rows, HEADS, HEAD_DIM)
    key_rows, value_rows = (
        lax.all_gather(local_keys, "seq", axis=1, tiled=True),
        lax.all_gather(local_values, "seq", axis=1, tiled=True),
    )
    masked = jnp.where(allowed[None, None], head_scores(queries, key_rows), -1e30)
    row_peak = jnp.max(masked, -1, keepdims=True)
    raised = jnp.exp(masked - row_peak)
    row_total = jnp.sum(raised, -1, keepdims=True)
    log_total = row_peak + jnp.log(row_total)
    attention = (raised / row_total).astype(jnp.bfloat16)
    attended = jnp.einsum(
        "shct,sthd->schd", attention, value_rows, preferred_element_type=jnp.float32
    )
    attended = attended.reshape(slots, rows, width).astype(jnp.bfloat16)
    middle = stream + jnp.einsum(
        "scd,de->sce", attended, matrix_out, preferred_element_type=jnp.float32
    )
    normed = norm_rows(middle, gain_b, shift_b).astype(jnp.bfloat16)
    hidden_up = jnp.einsum("scd,df->scf", normed, matrix_up, preferred_element_type=jnp.float32)
    active = gelu_exact(hidden_up).astype(jnp.bfloat16)
    output = middle + jnp.einsum(
        "scf,fd->scd", active, matrix_down, preferred_element_type=jnp.float32
    )
    kept = (
        stream,
        hidden,
        queries,
        key_rows,
        value_rows,
        log_total,
        attended,
        middle,
        normed,
        hidden_up,
        active,
    )
    return (output, kept)


def layer_backward(upstream, weights, kept, allowed):
    gain_a, shift_a, matrix_qkv, matrix_out, gain_b, shift_b, matrix_up, matrix_down = weights
    (
        stream,
        hidden,
        queries,
        key_rows,
        value_rows,
        log_total,
        attended,
        middle,
        normed,
        hidden_up,
        active,
    ) = kept
    slots, rows, width = stream.shape
    score_scale = 1.0 / math.sqrt(HEAD_DIM)
    back_out = upstream.astype(jnp.bfloat16)
    grad_down = jnp.einsum("scf,scd->fd", active, back_out, preferred_element_type=jnp.float32)
    back_active = jnp.einsum(
        "scd,fd->scf", back_out, matrix_down, preferred_element_type=jnp.float32
    )
    unused, gelu_pull = jax.vjp(gelu_exact, hidden_up)
    back_up = gelu_pull(back_active)[0].astype(jnp.bfloat16)
    grad_up = jnp.einsum("scd,scf->df", normed, back_up, preferred_element_type=jnp.float32)
    back_normed = jnp.einsum("scf,df->scd", back_up, matrix_up, preferred_element_type=jnp.float32)
    unused, norm_pull_two = jax.vjp(norm_rows, middle, gain_b, shift_b)
    back_middle, grad_gain_b, grad_shift_b = norm_pull_two(back_normed)
    back_middle = back_middle + upstream
    back_branch = back_middle.astype(jnp.bfloat16)
    grad_out = jnp.einsum("scd,sce->de", attended, back_branch, preferred_element_type=jnp.float32)
    back_attended = jnp.einsum(
        "sce,de->scd", back_branch, matrix_out, preferred_element_type=jnp.float32
    )
    back_attended = back_attended.astype(jnp.bfloat16).reshape(slots, rows, HEADS, HEAD_DIM)
    attention = jnp.where(
        allowed[None, None], jnp.exp(head_scores(queries, key_rows) - log_total), 0.0
    )
    back_attention = jnp.einsum(
        "schd,sthd->shct", back_attended, value_rows, preferred_element_type=jnp.float32
    )
    row_dot = jnp.sum(attention * back_attention, -1, keepdims=True)
    back_scores = (attention * (back_attention - row_dot)).astype(jnp.bfloat16)
    back_queries = (
        jnp.einsum("shct,sthd->schd", back_scores, key_rows, preferred_element_type=jnp.float32)
        * score_scale
    )
    back_keys = (
        jnp.einsum("shct,schd->sthd", back_scores, queries, preferred_element_type=jnp.float32)
        * score_scale
    )
    back_values = jnp.einsum(
        "shct,schd->sthd",
        attention.astype(jnp.bfloat16),
        back_attended,
        preferred_element_type=jnp.float32,
    )
    back_keys, back_values = (
        lax.psum_scatter(
            back_keys.astype(jnp.bfloat16), "seq", scatter_dimension=1, tiled=True
        ).astype(jnp.float32),
        lax.psum_scatter(
            back_values.astype(jnp.bfloat16), "seq", scatter_dimension=1, tiled=True
        ).astype(jnp.float32),
    )
    back_projected = jnp.concatenate(
        [
            back_queries.reshape(slots, rows, width).astype(jnp.bfloat16),
            back_keys.reshape(slots, rows, width).astype(jnp.bfloat16),
            back_values.reshape(slots, rows, width).astype(jnp.bfloat16),
        ],
        -1,
    )
    grad_qkv = jnp.einsum("scd,sce->de", hidden, back_projected, preferred_element_type=jnp.float32)
    back_hidden = jnp.einsum(
        "sce,de->scd", back_projected, matrix_qkv, preferred_element_type=jnp.float32
    )
    unused, norm_pull_one = jax.vjp(norm_rows, stream, gain_a, shift_a)
    back_stream, grad_gain_a, grad_shift_a = norm_pull_one(back_hidden)
    section_grads = (
        grad_gain_a,
        grad_shift_a,
        grad_qkv,
        grad_out,
        grad_gain_b,
        grad_shift_b,
        grad_up,
        grad_down,
    )
    return (back_stream + back_middle, section_grads)


def per_device(
    inputs,
    cotangent,
    task_table,
    type_counts,
    gain_one,
    bias_one,
    proj_qkv,
    proj_out,
    gain_two,
    bias_two,
    proj_up,
    proj_down,
):
    slots, rows, width = inputs.shape
    length = rows * lax.axis_size("seq")
    query_pos = lax.axis_index("seq") * rows + jnp.arange(rows, dtype=jnp.int32)
    every_pos = jnp.arange(length, dtype=jnp.int32)
    allowed = every_pos[None, :] <= query_pos[:, None]
    choose = (task_table[:, None] == jnp.arange(TASKS, dtype=jnp.int32)[None, :]).astype(
        jnp.float32
    )
    targets = (length - type_counts[:, 0]).astype(jnp.float32)
    totals = lax.psum(jnp.sum(choose * targets[:, None], 0), "dp")
    factor = jnp.sum(totals) / TASKS / totals
    seq_weight = jnp.sum(choose * factor[None, :], 1)
    target_mask = (query_pos[None, :] >= type_counts[:, 0:1]).astype(jnp.float32)
    upstream = cotangent.astype(jnp.float32) * (seq_weight[:, None] * target_mask)[:, :, None]
    stacked = (gain_one, bias_one, proj_qkv, proj_out, gain_two, bias_two, proj_up, proj_down)
    stream = inputs.astype(jnp.float32)
    kept_all = []
    for section_index in range(LAYERS):
        weights = tuple((weight[section_index] for weight in stacked))
        stream, kept = layer_forward(stream, weights, allowed)
        kept_all.append(kept)
    collected = []
    for section_index in reversed(range(LAYERS)):
        weights = tuple((weight[section_index] for weight in stacked))
        upstream, section_grads = layer_backward(
            upstream, weights, kept_all[section_index], allowed
        )
        collected.insert(0, section_grads)
    summed = tuple(
        (jnp.stack([section_grads[member] for section_grads in collected]) for member in range(8))
    )
    shares = lax.psum_scatter(summed, ("dp", "seq"), scatter_dimension=1, tiled=True)
    return (
        stream.astype(jnp.bfloat16),
        upstream,
        shares[0],
        shares[1],
        shares[2],
        shares[3],
        shares[4],
        shares[5],
        shares[6],
        shares[7],
    )


def solution(mesh):
    in_specs = (
        P("dp", "seq", None),
        P("dp", "seq", None),
        P("dp"),
        P("dp", None),
        P(),
        P(),
        P(),
        P(),
        P(),
        P(),
        P(),
        P(),
    )
    out_specs = (
        P("dp", "seq", None),
        P("dp", "seq", None),
        P(None, ("dp", "seq")),
        P(None, ("dp", "seq")),
        P(None, ("dp", "seq"), None),
        P(None, ("dp", "seq"), None),
        P(None, ("dp", "seq")),
        P(None, ("dp", "seq")),
        P(None, ("dp", "seq"), None),
        P(None, ("dp", "seq"), None),
    )
    return jax.shard_map(
        per_device, mesh=mesh, in_specs=in_specs, out_specs=out_specs, check_vma=False
    )
```

profile of v0, /device:TPU:0, one launch (start us, length us, event | category | flops | bytes accessed | tf_op | source)
XLA Modules:
  0.0 1238.4 jit_solution(10566881157136995330)
XLA Ops:
  11.7 4.4 convolution_convert_fusion.1
  19.4 29.9 %all-gather.7.cloned.1.call-done = bf16[2,1024,12,64]{1,3,2,0:T(8,128)(2,1)} async-done(((bf16[2,256,12,64]{1,3,2,0:T(8,128)(2,1)}), bf16[2,1024,12,64]{1,3,2,0:T(8,128)(2,1)}) %all-gather.7.cloned.1.call-update) | async-done | bytes 3145744 | tf_op jit(solution)/shard_map/all_gather | solution.py:47
  49.3 13.4 %select_reduce_fusion.1 = (f32[2,12,256]{2,1,0:T(8,128)S(1)}, f32[2,12,256,1024]{3,2,1,0:T(8,128)}) fusion(pred[256,1024]{1,0:T(8,128)(4,1)S(1)} %iota_compare_fusion, bf16[2,256,12,64]{1,3,2,0:T(8,128)(2,1)S(1)} %bitcast.174, bf16[2,1024,12,64]{1,3,2,0:T(8,128)(2,1)} %all-gather.7.cloned.1.call-done), kind=kOutput, calls=%fused_computation.11 | convolution fusion | flops 824174592 | bytes 29384704 | tf_op jit(solution)/shard_map/schd,sthd->shct/dot_general | solution.py:31
  62.7 11.7 fusion
  74.4 6.0 all-gather.5.cloned.1.call-done
  80.4 12.5 %fusion.90 = bf16[2,12,64,256]{3,2,1,0:T(8,128)(2,1)S(1)} fusion(bf16[2,1024,12,64]{1,3,2,0:T(8,128)(2,1)} %all-gather.5.cloned.1.call-done, f32[2,12,256,1024]{3,2,1,0:T(8,128)} %get-tuple-element.55, f32[2,12,256]{2,1,0:T(8,128)S(1)} %fusion, f32[2,12,256]{2,1,0:T(8,128)S(1)} %get-tuple-element.54, pred[256,1024]{1,0:T(8,128)(4,1)S(1)} %iota_compare_fusion), kind=kOutput, calls=%fused_computation.167 | convolution fusion | flops 837156864 | bytes 29409280 | tf_op jit(solution)/shard_map/shct,sthd->schd/dot_general | solution.py:56
  94.2 6.9 fusion.82
  101.2 15.4 %multiply_convert_fusion.5 = (bf16[2,256,3072]{2,1,0:T(8,128)(2,1)S(1)}, f32[2,256,3072]{2,1,0:T(8,128)}) fusion(f32[2,256,3072]{2,1,0:T(8,128)S(1)} %get-tuple-element.58, u8[256,3072]{1,0:T(8,128)(4,1)S(1)} %get-tuple-element.13, u8[256,3072]{1,0:T(8,128)(4,1)S(1)} %get-tuple-element.12), kind=kLoop, calls=%fused_computation.55 | loop fusion | flops 110100480 | bytes 17301504 | tf_op jit(solution)/shard_map/convert_element_type | solution.py:65
  116.6 6.2 fusion.134
  130.8 21.8 %psum.7 = f32[3]{0:T(128)S(1)} all-reduce(f32[3]{0:T(128)S(1)} %select_reduce_fusion.3), channel_id=1, replica_groups=mesh['dp'=8,'seq'=4] {'dp'}, use_global_device_ids=true, to_apply=%region_13.14 | all-reduce | flops 3 | bytes 24 | tf_op jit(solution)/shard_map/psum | solution.py:200
  158.4 13.1 %select_reduce_fusion = (f32[2,12,256]{2,1,0:T(8,128)S(1)}, f32[2,12,256,1024]{3,2,1,0:T(8,128)}) fusion(pred[256,1024]{1,0:T(8,128)(4,1)S(1)} %iota_compare_fusion, bf16[2,256,12,64]{1,3,2,0:T(8,128)(2,1)S(1)} %bitcast.176, bf16[2,1024,12,64]{1,3,2,0:T(8,128)(2,1)} %all-gather.11.cloned.1.call-done), kind=kOutput, calls=%fused_computation.10 | convolution fusion | flops 824174592 | bytes 29384704 | tf_op jit(solution)/shard_map/schd,sthd->shct/dot_general | solution.py:31
  171.5 11.7 fusion.1
  183.2 6.1 all-gather.9.cloned.1.call-done
  189.3 12.8 %fusion.89 = bf16[2,12,64,256]{3,2,1,0:T(8,128)(2,1)S(1)} fusion(bf16[2,1024,12,64]{1,3,2,0:T(8,128)(2,1)} %all-gather.9.cloned.1.call-done, f32[2,12,256,1024]{3,2,1,0:T(8,128)} %get-tuple-element.62, f32[2,12,256]{2,1,0:T(8,128)S(1)} %fusion.1, f32[2,12,256]{2,1,0:T(8,128)S(1)} %get-tuple-element.61, pred[256,1024]{1,0:T(8,128)(4,1)S(1)} %iota_compare_fusion), kind=kOutput, calls=%fused_computation.166 | convolution fusion | flops 837156864 | bytes 29409280 | tf_op jit(solution)/shard_map/shct,sthd->schd/dot_general | solution.py:56
  203.4 7.1 fusion.83
  210.5 15.0 %multiply_convert_fusion.4 = (bf16[2,256,3072]{2,1,0:T(8,128)(2,1)}, f32[2,256,3072]{2,1,0:T(8,128)S(1)}) fusion(f32[2,256,3072]{2,1,0:T(8,128)S(1)} %get-tuple-element.65, u8[256,3072]{1,0:T(8,128)(4,1)S(1)} %get-tuple-element.11, u8[256,3072]{1,0:T(8,128)(4,1)S(1)} %get-tuple-element.10), kind=kLoop, calls=%fused_computation.42 | loop fusion | flops 110100480 | bytes 17301504 | tf_op jit(solution)/shard_map/convert_element_type | solution.py:65
  225.5 8.0 add_convert_fusion.1
  233.5 6.9 multiply_reduce_fusion.2
  246.5 19.1 %multiply_reduce_fusion.1 = (f32[2,12,256]{2,1,0:T(8,128)S(1)}, f32[2,12,256,1024]{3,2,1,0:T(8,128)}) fusion(f32[2,12,256,1024]{3,2,1,0:T(8,128)} %get-tuple-element.62, f32[2,12,256]{2,1,0:T(8,128)S(1)} %log_add_fusion, pred[256,1024]{1,0:T(8,128)(4,1)S(1)} %iota_compare_fusion, bf16[2,256,12,64]{1,3,2,0:T(8,128)(2,1)S(1)} %bitcast.188, ...), kind=kOutput, calls=%fused_computation.3 | convolution fusion | flops 836757504 | bytes 54575104 | tf_op jit(solution)/shard_map/schd,sthd->shct/dot_general | solution.py:123
  265.5 16.9 %multiply_convert_fusion.1 = bf16[2,12,256,1024]{3,2,1,0:T(8,128)(2,1)S(1)} fusion(f32[2,12,256,1024]{3,2,1,0:T(8,128)} %get-tuple-element.68, f32[2,12,256,1024]{3,2,1,0:T(8,128)} %get-tuple-element.62, f32[2,12,256]{2,1,0:T(8,128)S(1)} %get-tuple-element.67, f32[2,12,256]{2,1,0:T(8,128)S(1)} %log_add_fusion, pred[256,1024]{1,0:T(8,128)(4,1)S(1)} %iota_compare_fusion), kind=kLoop, calls=%fused_computation.2 | loop fusion | flops 37748736 | bytes 63225856 | tf_op jit(solution)/shard_map/convert_element_type | solution.py:127
  282.5 4.5 copy-done.1
  291.0 14.1 %convert_bitcast_fusion.1 = bf16[2,1024,12,64]{1,3,2,0:T(8,128)(2,1)} fusion(bf16[2,256,12,64]{1,3,2,0:T(8,128)(2,1)S(1)} %bitcast.189, f32[2,12,256,1024]{3,2,1,0:T(8,128)} %get-tuple-element.62, f32[2,12,256]{2,1,0:T(8,128)S(1)} %log_add_fusion, pred[256,1024]{1,0:T(8,128)(4,1)S(1)} %iota_compare_fusion), kind=kOutput, calls=%fused_computation.110 | convolution fusion | flops 832045056 | bytes 29384704 | tf_op jit(solution)/shard_map/shct,schd->sthd/dot_general | solution.py:136
  305.3 10.0 multiply_convert_fusion.7
  315.5 13.5 %reduce-scatter.13.cloned.1.call-done = bf16[2,256,12,64]{1,3,2,0:T(8,128)(2,1)} async-done(((bf16[2,1024,12,64]{1,3,2,0:T(8,128)(2,1)}), bf16[2,256,12,64]{1,3,2,0:T(8,128)(2,1)}) %reduce-scatter.13.cloned.1.call-update) | async-done | bytes 786448 | tf_op jit(solution)/shard_map/reduce_scatter | solution.py:143
  330.4 39.1 %reduce-scatter.15.cloned.1.call-done = bf16[2,256,12,64]{1,3,2,0:T(8,128)(2,1)} async-done(((bf16[2,1024,12,64]{1,3,2,0:T(8,128)(2,1)}), bf16[2,256,12,64]{1,3,2,0:T(8,128)(2,1)}) %reduce-scatter.15.cloned.1.call-update) | async-done | bytes 786448 | tf_op jit(solution)/shard_map/reduce_scatter | solution.py:146
  371.8 5.1 fusion.126
  379.4 9.5 add_convert_fusion
  389.0 4.9 multiply_reduce_fusion.3
  400.9 19.2 %multiply_reduce_fusion = (f32[2,12,256]{2,1,0:T(8,128)S(1)}, f32[2,12,256,1024]{3,2,1,0:T(8,128)}) fusion(f32[2,12,256,1024]{3,2,1,0:T(8,128)} %get-tuple-element.55, f32[2,12,256]{2,1,0:T(8,128)S(1)} %log_add_fusion.1, pred[256,1024]{1,0:T(8,128)(4,1)S(1)} %iota_compare_fusion, bf16[2,256,12,64]{1,3,2,0:T(8,128)(2,1)} %bitcast.186, ...), kind=kOutput, calls=%fused_computation.1 | convolution fusion | flops 836757504 | bytes 54575104 | tf_op jit(solution)/shard_map/schd,sthd->shct/dot_general | solution.py:123
  420.0 17.4 %multiply_convert_fusion = bf16[2,12,256,1024]{3,2,1,0:T(8,128)(2,1)S(1)} fusion(f32[2,12,256,1024]{3,2,1,0:T(8,128)} %get-tuple-element.72, f32[2,12,256,1024]{3,2,1,0:T(8,128)} %get-tuple-element.55, f32[2,12,256]{2,1,0:T(8,128)S(1)} %get-tuple-element.71, f32[2,12,256]{2,1,0:T(8,128)S(1)} %log_add_fusion.1, pred[256,1024]{1,0:T(8,128)(4,1)S(1)} %iota_compare_fusion), kind=kLoop, calls=%fused_computation | loop fusion | flops 37748736 | bytes 63225856 | tf_op jit(solution)/shard_map/convert_element_type | solution.py:127
  437.4 4.4 copy-done
  445.9 13.9 %convert_bitcast_fusion = bf16[2,1024,12,64]{1,3,2,0:T(8,128)(2,1)} fusion(bf16[2,256,12,64]{1,3,2,0:T(8,128)(2,1)} %bitcast.187, f32[2,12,256,1024]{3,2,1,0:T(8,128)} %get-tuple-element.55, f32[2,12,256]{2,1,0:T(8,128)S(1)} %log_add_fusion.1, pred[256,1024]{1,0:T(8,128)(4,1)S(1)} %iota_compare_fusion), kind=kOutput, calls=%fused_computation.109 | convolution fusion | flops 832045056 | bytes 29384704 | tf_op jit(solution)/shard_map/shct,schd->sthd/dot_general | solution.py:136
  466.7 5.0 convolution_bitcast_fusion.2
  474.4 6.7 pad_maximum_fusion.1
  481.9 5.4 convolution_bitcast_fusion.4
  490.2 8.0 pad_maximum_fusion
  498.4 10.4 multiply_convert_fusion.6
  511.1 6.7 convolution_bitcast_fusion
  519.3 5.4 reduce-scatter.19.cloned.1.call-done
  526.1 6.8 convolution_bitcast_fusion.1
  532.9 11.1 pad_maximum_fusion.2
  545.5 7.1 add_convert_fusion.2
  552.8 4.6 fusion.125
  558.6 40.0 %all-reduce.4 = (f32[2,768]{1,0:T(2,128)S(1)}, f32[2,768]{1,0:T(2,128)S(1)}, f32[2,768]{1,0:T(2,128)S(1)}, f32[2,768]{1,0:T(2,128)S(1)}) all-reduce(f32[2,768]{1,0:T(2,128)S(1)} %pad_maximum_fusion.10, f32[2,768]{1,0:T(2,128)S(1)} %pad_maximum_fusion.11, ...), channel_id=6, replica_groups=mesh['dp'=8,'seq'=4] {'dp','seq'}, use_global_device_ids=true, to_apply=%region_32.33.clone | all-reduce | flops 6144 | bytes 49152
  604.5 33.3 %reduce-scatter.23.cloned.1.call-done = f32[2,24,768]{2,1,0:T(8,128)} async-done(((f32[2,768,768]{2,1,0:T(8,128)}), f32[2,24,768]{2,1,0:T(8,128)}) %reduce-scatter.23.cloned.1.call-update) | async-done | bytes 147472 | tf_op jit(solution)/shard_map/reduce_scatter | solution.py:222
  637.8 212.1 %reduce-scatter.27.cloned.1.call-done = f32[2,96,768]{2,1,0:T(8,128)} async-done(((f32[2,3072,768]{2,1,0:T(8,128)}), f32[2,96,768]{2,1,0:T(8,128)}) %reduce-scatter.27.cloned.1.call-update) | async-done | bytes 589840 | tf_op jit(solution)/shard_map/reduce_scatter | solution.py:222
  849.9 212.0 %reduce-scatter.25.cloned.1.call-done = f32[2,24,3072]{2,1,0:T(8,128)} async-done(((f32[2,768,3072]{2,1,0:T(8,128)}), f32[2,24,3072]{2,1,0:T(8,128)}) %reduce-scatter.25.cloned.1.call-update) | async-done | bytes 589840 | tf_op jit(solution)/shard_map/reduce_scatter | solution.py:222
  1062.0 169.3 %reduce-scatter.21.cloned.1.call-done = f32[2,24,2304]{2,1,0:T(8,128)} async-done(((f32[2,768,2304]{2,1,0:T(8,128)}), f32[2,24,2304]{2,1,0:T(8,128)}) %reduce-scatter.21.cloned.1.call-update) | async-done | bytes 442384 | tf_op jit(solution)/shard_map/reduce_scatter | solution.py:222
  (285 shorter events, 77.8 us)
Async XLA Ops:
  7.2 42.1 %all-gather.7.cloned.1.call-start = ((), (), s32[]{:S(2)}) async-start(), calls=%async_computation.9 | async-start | bytes 3932160 | tf_op jit(solution)/shard_map/all_gather | solution.py:47
  11.7 111.5 %copy-start.42 = (f32[768]{0:T(1024)}, f32[768]{0:T(1024)S(1)}, u32[]{:S(2)}) copy-start(f32[768]{0:T(1024)S(1)} %get-tuple-element.34) | copy-start | bytes 9220
  17.5 62.9 %all-gather.5.cloned.1.call-start = ((), (), s32[]{:S(2)}) async-start(), calls=%async_computation.8 | async-start | bytes 3932160 | tf_op jit(solution)/shard_map/all_gather | solution.py:48
  18.8 139.6 %all-gather.11.cloned.1.call-start = ((), (), s32[]{:S(2)}) async-start(), calls=%async_computation.11 | async-start | bytes 3932160 | tf_op jit(solution)/shard_map/all_gather | solution.py:47
  19.1 43.6 %copy-start.12 = (bf16[2,256,768]{1,2,0:T(8,128)(2,1)}, bf16[2,256,768]{1,2,0:T(8,128)(2,1)S(1)}, u32[]{:S(2)}) copy-start(bf16[2,256,768]{1,2,0:T(8,128)(2,1)S(1)} %copy.93) | copy-start | bytes 2359300
  19.2 75.0 %copy-start.59 = (f32[768]{0:T(1024)}, f32[768]{0:T(1024)S(1)}, u32[]{:S(2)}) copy-start(f32[768]{0:T(1024)S(1)} %get-tuple-element.74) | copy-start | bytes 9220
  19.2 75.0 %copy-start.71 = (f32[768]{0:T(1024)}, f32[768]{0:T(1024)S(1)}, u32[]{:S(2)}) copy-start(f32[768]{0:T(1024)S(1)} %get-tuple-element.31) | copy-start | bytes 9220
  19.2 184.2 %copy-start.73 = (f32[768]{0:T(1024)}, f32[768]{0:T(1024)S(1)}, u32[]{:S(2)}) copy-start(f32[768]{0:T(1024)S(1)} %get-tuple-element.30) | copy-start | bytes 9220
  19.2 221.2 %copy-start.61 = (f32[768]{0:T(1024)}, f32[768]{0:T(1024)S(1)}, u32[]{:S(2)}) copy-start(f32[768]{0:T(1024)S(1)} %get-tuple-element.75) | copy-start | bytes 9220
  62.7 17.7 %copy-start.36 = (f32[2,12,256]{2,1,0:T(8,128)}, f32[2,12,256]{2,1,0:T(8,128)S(1)}, u32[]{:S(2)}) copy-start(f32[2,12,256]{2,1,0:T(8,128)S(1)} %get-tuple-element.54) | copy-start | bytes 73732
  74.4 18.5 %copy-start.38 = (f32[2,12,256]{2,1,0:T(8,128)}, f32[2,12,256]{2,1,0:T(8,128)S(1)}, u32[]{:S(2)}) copy-start(f32[2,12,256]{2,1,0:T(8,128)S(1)} %fusion) | copy-start | bytes 73732
  74.4 18.5 %copy-start.10 = (bf16[2,256,768]{2,1,0:T(8,128)(2,1)S(1)}, bf16[2,256,768]{2,1,0:T(8,128)(2,1)}, u32[]{:S(2)}) copy-start(bf16[2,256,768]{2,1,0:T(8,128)(2,1)} %param.12) | copy-start | bytes 2359300
  74.4 18.5 %copy-start.32 = (bf16[2,768,768]{2,1,0:T(8,128)(2,1)S(1)}, bf16[2,768,768]{2,1,0:T(8,128)(2,1)}, u32[]{:S(2)}) copy-start(bf16[2,768,768]{2,1,0:T(8,128)(2,1)} %param.19) | copy-start | bytes 7077892
  93.8 22.8 %copy-start.15 = (f32[2,256,768]{2,1,0:T(8,128)}, f32[2,256,768]{2,1,0:T(8,128)S(1)}, u32[]{:S(2)}) copy-start(f32[2,256,768]{2,1,0:T(8,128)S(1)} %get-tuple-element.57) | copy-start | bytes 4718596
  101.2 15.4 %copy-start.14 = (f32[2,256,3072]{2,1,0:T(8,128)}, f32[2,256,3072]{2,1,0:T(8,128)S(1)}, u32[]{:S(2)}) copy-start(f32[2,256,3072]{2,1,0:T(8,128)S(1)} %get-tuple-element.58) | copy-start | bytes 18874372
  101.2 22.6 %slice-start.3 = ((s8[7077888]{0:T(1024)(128)(4,1)}), s8[2883584]{0:T(1024)(128)(4,1)S(1)}, s32[]{:S(2)}) async-start(s8[7077888]{0:T(1024)(128)(4,1)} %bitcast.198), calls=%async_computation.23 | async-start | bytes 5767168
  129.3 60.0 %all-gather.9.cloned.1.call-start = ((), (), s32[]{:S(2)}) async-start(), calls=%async_computation.10 | async-start | bytes 3932160 | tf_op jit(solution)/shard_map/all_gather | solution.py:48
  130.5 198.5 %reduce-scatter.13.cloned.1.call-start = ((), (), s32[]{:S(2)}) async-start(), calls=%async_computation.12 | async-start | bytes 3932160 | tf_op jit(solution)/shard_map/reduce_scatter | solution.py:143
  189.3 12.8 %copy-start.33 = (bf16[2,768,768]{2,1,0:T(8,128)(2,1)S(1)}, bf16[2,768,768]{2,1,0:T(8,128)(2,1)}, u32[]{:S(2)}) copy-start(bf16[2,768,768]{2,1,0:T(8,128)(2,1)} %param.19) | copy-start | bytes 7077892
  203.0 37.3 %copy-start.6 = (f32[2,256,768]{2,1,0:T(8,128)}, f32[2,256,768]{2,1,0:T(8,128)S(1)}, u32[]{:S(2)}) copy-start(f32[2,256,768]{2,1,0:T(8,128)S(1)} %get-tuple-element.64) | copy-start | bytes 4718596
  203.0 37.3 %copy-start.50 = (f32[2,256]{1,0:T(2,128)}, f32[2,256]{1,0:T(2,128)S(1)}, u32[]{:S(2)}) copy-start(f32[2,256]{1,0:T(2,128)S(1)} %broadcast_multiply_fusion) | copy-start | bytes 6148
  203.4 37.0 %copy-start.65 = (f32[2,256]{1,0:T(2,128)}, f32[2,256]{1,0:T(2,128)S(1)}, u32[]{:S(2)}) copy-start(f32[2,256]{1,0:T(2,128)S(1)} %fusion.112) | copy-start | bytes 6148
  210.5 15.0 %copy-start.21 = (bf16[2,256,768]{2,1,0:T(8,128)(2,1)S(1)}, bf16[2,256,768]{2,1,0:T(8,128)(2,1)}, u32[]{:S(2)}) copy-start(bf16[2,256,768]{2,1,0:T(8,128)(2,1)} %param.13) | copy-start | bytes 2359300
  290.9 14.3 %copy-start.37 = (f32[2,12,256]{2,1,0:T(8,128)S(1)}, f32[2,12,256]{2,1,0:T(8,128)}, u32[]{:S(2)}) copy-start(f32[2,12,256]{2,1,0:T(8,128)} %copy-done.36) | copy-start | bytes 73732
  291.0 14.3 %copy-start.39 = (f32[2,12,256]{2,1,0:T(8,128)S(1)}, f32[2,12,256]{2,1,0:T(8,128)}, u32[]{:S(2)}) copy-start(f32[2,12,256]{2,1,0:T(8,128)} %copy-done.38) | copy-start | bytes 73732
  291.0 78.6 %reduce-scatter.15.cloned.1.call-start = ((), (), s32[]{:S(2)}) async-start(), calls=%async_computation.13 | async-start | bytes 3932160 | tf_op jit(solution)/shard_map/reduce_scatter | solution.py:146
  305.2 212.7 %reduce-scatter.17.cloned.1.call-start = ((), (), s32[]{:S(2)}) async-start(), calls=%async_computation.14 | async-start | bytes 3932160 | tf_op jit(solution)/shard_map/reduce_scatter | solution.py:143
  315.5 61.4 %copy-start.19 = (bf16[2,256,768]{2,1,0:T(8,128)(2,1)}, bf16[2,256,768]{2,1,0:T(8,128)(2,1)S(1)}, u32[]{:S(2)}) copy-start(bf16[2,256,768]{2,1,0:T(8,128)(2,1)S(1)} %copy.101) | copy-start | bytes 2359300
  330.4 46.5 %copy-start.20 = (bf16[2,256,768]{2,1,0:T(8,128)(2,1)}, bf16[2,256,768]{2,1,0:T(8,128)(2,1)S(1)}, u32[]{:S(2)}) copy-start(bf16[2,256,768]{2,1,0:T(8,128)(2,1)S(1)} %copy.102) | copy-start | bytes 2359300
  378.3 10.6 slice-start
  379.3 9.6 copy-start.16
  379.3 9.6 copy-start.49
  379.3 9.6 copy-start.60
  379.3 9.6 copy-start.64
  420.0 21.9 %copy-start.13 = (bf16[2,256,768]{1,2,0:T(8,128)(2,1)S(1)}, bf16[2,256,768]{1,2,0:T(8,128)(2,1)}, u32[]{:S(2)}) copy-start(bf16[2,256,768]{1,2,0:T(8,128)(2,1)} %copy-done.12) | copy-start | bytes 2359300
  445.9 78.8 %reduce-scatter.19.cloned.1.call-start = ((), (), s32[]{:S(2)}) async-start(), calls=%async_computation.15 | async-start | bytes 3932160 | tf_op jit(solution)/shard_map/reduce_scatter | solution.py:146
  459.8 178.0 %reduce-scatter.23.cloned.1.call-start = ((), (), s32[]{:S(2)}) async-start(), calls=%async_computation.17 | async-start | bytes 4866048 | tf_op jit(solution)/shard_map/reduce_scatter | solution.py:222
  466.6 383.3 %reduce-scatter.27.cloned.1.call-start = ((), (), s32[]{:S(2)}) async-start(), calls=%async_computation.19 | async-start | bytes 19464192 | tf_op jit(solution)/shard_map/reduce_scatter | solution.py:222
  481.2 580.8 %reduce-scatter.25.cloned.1.call-start = ((), (), s32[]{:S(2)}) async-start(), calls=%async_computation.18 | async-start | bytes 19464192 | tf_op jit(solution)/shard_map/reduce_scatter | solution.py:222
  498.2 12.9 %copy-start.43 = (f32[768]{0:T(1024)S(1)}, f32[768]{0:T(1024)}, u32[]{:S(2)}) copy-start(f32[768]{0:T(1024)} %copy-done.42) | copy-start | bytes 9220
  498.2 733.1 %reduce-scatter.21.cloned.1.call-start = ((), (), s32[]{:S(2)}) async-start(), calls=%async_computation.16 | async-start | bytes 14598144 | tf_op jit(solution)/shard_map/reduce_scatter | solution.py:222
  511.1 14.9 %copy-start.41 = (f32[768]{0:T(1024)S(1)}, f32[768]{0:T(1024)}, u32[]{:S(2)}) copy-start(f32[768]{0:T(1024)} %copy-done.40) | copy-start | bytes 9220
  511.1 14.9 %copy-start.45 = (f32[2,256]{1,0:T(2,128)S(1)}, f32[2,256]{1,0:T(2,128)}, u32[]{:S(2)}) copy-start(f32[2,256]{1,0:T(2,128)} %copy-done.44) | copy-start | bytes 6148
  511.1 15.0 %copy-start.47 = (f32[2,256]{1,0:T(2,128)S(1)}, f32[2,256]{1,0:T(2,128)}, u32[]{:S(2)}) copy-start(f32[2,256]{1,0:T(2,128)} %copy-done.46) | copy-start | bytes 6148
  511.1 15.0 %copy-start.70 = (f32[768]{0:T(1024)S(1)}, f32[768]{0:T(1024)}, u32[]{:S(2)}) copy-start(f32[768]{0:T(1024)} %copy-done.69) | copy-start | bytes 9220
  519.3 13.6 %copy-start.27 = (bf16[2,256,768]{2,1,0:T(8,128)(2,1)}, bf16[2,256,768]{2,1,0:T(8,128)(2,1)S(1)}, u32[]{:S(2)}) copy-start(bf16[2,256,768]{2,1,0:T(8,128)(2,1)S(1)} %copy.106) | copy-start | bytes 2359300
  526.1 17.9 %copy-start.29 = (bf16[2,256,768]{2,1,0:T(8,128)(2,1)}, bf16[2,256,768]{2,1,0:T(8,128)(2,1)S(1)}, u32[]{:S(2)}) copy-start(bf16[2,256,768]{2,1,0:T(8,128)(2,1)S(1)} %copy.107) | copy-start | bytes 2359300
  552.8 48.3 %copy-start.3 = (f32[2,256,768]{2,1,0:T(8,128)S(1)}, f32[2,256,768]{2,1,0:T(8,128)}, u32[]{:S(2)}) copy-start(f32[2,256,768]{2,1,0:T(8,128)} %copy-done.2) | copy-start | bytes 4718596
  (50 other events, 230.1 us)
Sparse Core Ops, SparseCore 0:
  17.6 31.6 all-gather.6
  51.4 28.9 all-gather.4
  129.4 28.9 all-gather.10
  160.3 28.9 all-gather.8
  291.1 37.9 reduce-scatter.12
  331.6 37.9 reduce-scatter.14
  446.0 37.9 reduce-scatter.16
  486.7 37.9 reduce-scatter.18
  530.7 107.0 reduce-scatter.22
  645.8 204.1 reduce-scatter.26
  858.1 203.8 reduce-scatter.24
  1069.4 161.8 reduce-scatter.20
where the time goes:
time: 1240 us
  waiting for transfers between devices  731 us (59%)
  matrix products  258 us (21%)
  other arithmetic  130 us (10%)
  blocking collectives  61.7 us (5%)
  local copies, waits for them, and re-layouts  40.7 us (3%)
  between operations  16.4 us (1%)
    reduce_scatter x4, waiting for transfers between devices, per_device(): lax.psum_scatter(summed, ('dp', 'seq'), scatter_dimension=1, tiled=True)  627 us
    reduce_scatter x2, waiting for transfers between devices, layer_backward(): lax.psum_scatter(back_values.astype(jnp.bfloat16), 'seq', scatter_dimensi...  44.4 us
    unnamed x1, blocking collectives  40 us
    dot_general x2, matrix products, layer_backward(): jnp.einsum('schd,sthd->shct', back_attended, value_rows, preferred_elemen...  38.2 us
    convert_element_type x2, other arithmetic, layer_backward(): back_scores = (attention * (back_attention - row_dot)).astype(jnp.bfloat16)  34.4 us
    all_gather x2, waiting for transfers between devices, layer_forward(): lax.all_gather(local_keys, 'seq', axis=1, tiled=True)  33.8 us
    convert_element_type x2, other arithmetic, layer_forward(): active = gelu_exact(hidden_up).astype(jnp.bfloat16)  30.4 us
    another operation x8, other arithmetic, per_device(): jnp.stack([section_grads[member] for section_grads in collected])  28.3 us
  transfers between devices with their start and end apart: 12, of which 11 were waited for; matrix products, arithmetic and copies ran while one was open for 15% of the time, Pallas kernels for 0%

commit v1 on v0

v1 whole, which is shorter than its diff:
```python
import functools
import math

import jax
import jax.numpy as jnp
import numpy as np
from jax import lax
from jax.experimental import pallas as pl
from jax.experimental.pallas import tpu as pltpu
from jax.sharding import PartitionSpec as P

HEADS = 12
HEAD_DIM = 64
LAYERS = 2
TASKS = 3
AXES = ("dp", "seq")
F32 = jnp.float32
BF16 = jnp.bfloat16
epsilon = 1e-05
VMEM_BYTES = 56 * 1024 * 1024


def dot_nn(a, b):
    return lax.dot_general(a, b, (((1,), (0,)), ((), ())), preferred_element_type=F32)


def dot_nt(a, b):
    return lax.dot_general(a, b, (((1,), (1,)), ((), ())), preferred_element_type=F32)


def dot_tn(a, b):
    return lax.dot_general(a, b, (((0,), (0,)), ((), ())), preferred_element_type=F32)


def norm_rows(rows_in, gain_row, shift_row):
    average = jnp.mean(rows_in, -1, keepdims=True)
    centred = rows_in - average
    spread = jnp.mean(centred * centred, -1, keepdims=True)
    return centred * lax.rsqrt(spread + epsilon) * gain_row + shift_row


def gelu_and_slope(x):
    z = jnp.abs(x) * 0.7071067811865476
    d = 1.0 + 0.3275911 * z
    t = pl.reciprocal(d, approx=True)
    t = t * (2.0 - d * t)
    poly = t * (
        0.254829592
        + t * (-0.284496736 + t * (1.421413741 + t * (-1.453152027 + t * 1.061405429)))
    )
    bell = jnp.exp(-0.5 * x * x)
    tail = 0.5 * poly * bell
    below = jnp.where(x >= 0.0, 1.0 - tail, tail)
    return x * below, below + x * bell * 0.3989422804014327


def pair_lists(variant):
    if variant == 0:
        return [[(0, 0, True)], [(0, 0, False), (1, 0, False), (1, 1, False), (0, 1, True)]]
    return [[(1, 0, False), (0, 0, True)], [(0, 0, False), (1, 0, False), (0, 1, True)]]


def head_masks(scale):
    lane = lax.broadcasted_iota(jnp.int32, (1, 2 * HEAD_DIM), 1)
    first = jnp.where(lane < HEAD_DIM, scale, 0.0)
    return first.astype(BF16), (scale - first).astype(BF16)


def attention_forward_kernel(meta, q_ref, ko_ref, vo_ref, kx_ref, vx_ref, out_ref, lse_ref):
    rows = q_ref.shape[0] // 2
    masks = head_masks(1.0 / math.sqrt(HEAD_DIM))
    keys = (ko_ref, kx_ref)
    values = (vo_ref, vx_ref)

    def run(variant):
        below = lax.broadcasted_iota(jnp.int32, (rows, rows), 1) <= lax.broadcasted_iota(
            jnp.int32, (rows, rows), 0
        )
        lane = lax.broadcasted_iota(jnp.int32, (rows, 2 * HEAD_DIM), 1)
        for block, pairs in enumerate(pair_lists(variant)):
            span = pl.ds(block * rows, rows)
            q = q_ref[span, :]
            results, logs = [], []
            for head in range(2):
                qm = q * masks[head]
                scores = []
                for source, kblock, diagonal in pairs:
                    part = dot_nt(qm, keys[source][pl.ds(kblock * rows, rows), :])
                    scores.append(jnp.where(below, part, -1e30) if diagonal else part)
                peak = functools.reduce(jnp.maximum, scores)
                peak = jnp.max(peak, -1, keepdims=True)
                total, acc = None, None
                for part, (source, kblock, diagonal) in zip(scores, pairs):
                    raised = jnp.exp(part - peak)
                    total = raised if total is None else total + raised
                    term = dot_nn(raised.astype(BF16), values[source][pl.ds(kblock * rows, rows), :])
                    acc = term if acc is None else acc + term
                total = jnp.sum(total, -1, keepdims=True)
                results.append(acc / total)
                logs.append(peak + jnp.log(total))
            out_ref[span, :] = jnp.where(lane < HEAD_DIM, results[0], results[1]).astype(BF16)
            packed = jnp.where(lane == 0, logs[0], logs[1])
            lse_ref[0, :, span] = packed.T[:8, :]

    @pl.when(meta[0] == 0)
    def _():
        run(0)

    @pl.when(meta[0] == 1)
    def _():
        run(1)


def attention_forward(meta, projected, other):
    tokens = projected.shape[0]
    pairs = HEADS // 2
    wide = 2 * HEAD_DIM

    def at(offset):
        return pl.BlockSpec((tokens, wide), lambda g, m: (0, offset + g))

    return pl.pallas_call(
        attention_forward_kernel,
        grid_spec=pltpu.PrefetchScalarGridSpec(
            num_scalar_prefetch=1,
            grid=(pairs,),
            in_specs=[at(0), at(pairs), at(2 * pairs), at(0), at(pairs)],
            out_specs=[at(0), pl.BlockSpec((1, 8, tokens), lambda g, m: (g, 0, 0))],
        ),
        out_shape=[
            jax.ShapeDtypeStruct((tokens, HEADS * HEAD_DIM), BF16),
            jax.ShapeDtypeStruct((pairs, 8, tokens), F32),
        ],
        compiler_params=pltpu.CompilerParams(vmem_limit_bytes=VMEM_BYTES),
        cost_estimate=pl.CostEstimate(flops=8_000_000_000, bytes_accessed=4_000_000, transcendentals=4_000_000),
        name="attention_forward",
    )(meta, projected, projected, projected, other, other)


def attention_backward_kernel(
    meta, q_ref, ko_ref, vo_ref, kx_ref, vx_ref, do_ref, o_ref, lse_ref,
    dq_ref, dko_ref, dvo_ref, dkx_ref, dvx_ref,
):
    rows = q_ref.shape[0] // 2
    scale = 1.0 / math.sqrt(HEAD_DIM)
    scaled = head_masks(scale)
    plain = head_masks(1.0)
    keys = (ko_ref, kx_ref)
    values = (vo_ref, vx_ref)
    dkeys = (dko_ref, dkx_ref)
    dvalues = (dvo_ref, dvx_ref)
    product = (do_ref[...].astype(F32) * o_ref[...].astype(F32)).T
    dots = (
        jnp.sum(product[:HEAD_DIM], 0, keepdims=True),
        jnp.sum(product[HEAD_DIM:], 0, keepdims=True),
    )
    logs = lse_ref[0]

    def run(variant):
        below = lax.broadcasted_iota(jnp.int32, (rows, rows), 0) <= lax.broadcasted_iota(
            jnp.int32, (rows, rows), 1
        )
        dk_acc, dv_acc = {}, {}
        for block, pairs in enumerate(pair_lists(variant)):
            span = slice(block * rows, (block + 1) * rows)
            q, do = q_ref[span, :], do_ref[span, :]
            dq = None
            for head in range(2):
                qm, dom = q * scaled[head], do * plain[head]
                log_row = logs[head : head + 1, span]
                dot_row = dots[head][:, span]
                for source, kblock, diagonal in pairs:
                    where = pl.ds(kblock * rows, rows)
                    k, v = keys[source][where, :], values[source][where, :]
                    raised = jnp.exp(dot_nt(k, qm) - log_row)
                    if diagonal:
                        raised = jnp.where(below, raised, 0.0)
                    slope = (raised * (dot_nt(v, dom) - dot_row)).astype(BF16)
                    term_v = dot_nn(raised.astype(BF16), dom)
                    term_k = dot_nn(slope, qm)
                    term_q = dot_tn(slope, k * scaled[head])
                    slot = (source, kblock)
                    dv_acc[slot] = dv_acc[slot] + term_v if slot in dv_acc else term_v
                    dk_acc[slot] = dk_acc[slot] + term_k if slot in dk_acc else term_k
                    dq = term_q if dq is None else dq + term_q
            dq_ref[span, :] = dq.astype(BF16)
        for source in range(2):
            for kblock in range(2):
                span = slice(kblock * rows, (kblock + 1) * rows)
                slot = (source, kblock)
                if slot in dk_acc:
                    dkeys[source][span, :] = dk_acc[slot].astype(dkeys[source].dtype)
                    dvalues[source][span, :] = dv_acc[slot].astype(dvalues[source].dtype)
                else:
                    dkeys[source][span, :] = jnp.zeros((rows, 2 * HEAD_DIM), dkeys[source].dtype)
                    dvalues[source][span, :] = jnp.zeros((rows, 2 * HEAD_DIM), dvalues[source].dtype)

    @pl.when(meta[0] == 0)
    def _():
        run(0)

    @pl.when(meta[0] == 1)
    def _():
        run(1)


def attention_backward(meta, projected, other, back_attended, attended, logs):
    tokens = projected.shape[0]
    pairs = HEADS // 2
    wide = 2 * HEAD_DIM
    width = HEADS * HEAD_DIM

    def at(offset):
        return pl.BlockSpec((tokens, wide), lambda g, m: (0, offset + g))

    return pl.pallas_call(
        attention_backward_kernel,
        grid_spec=pltpu.PrefetchScalarGridSpec(
            num_scalar_prefetch=1,
            grid=(pairs,),
            in_specs=[at(0), at(pairs), at(2 * pairs), at(0), at(pairs), at(0), at(0),
                      pl.BlockSpec((1, 8, tokens), lambda g, m: (g, 0, 0))],
            out_specs=[at(0)] * 5,
        ),
        out_shape=[
            jax.ShapeDtypeStruct((tokens, width), BF16),
            jax.ShapeDtypeStruct((tokens, width), F32),
            jax.ShapeDtypeStruct((tokens, width), F32),
            jax.ShapeDtypeStruct((tokens, width), BF16),
            jax.ShapeDtypeStruct((tokens, width), BF16),
        ],
        compiler_params=pltpu.CompilerParams(vmem_limit_bytes=VMEM_BYTES),
        cost_estimate=pl.CostEstimate(flops=16_000_000_000, bytes_accessed=9_000_000, transcendentals=4_000_000),
        name="attention_backward",
    )(meta, projected, projected, projected, other, other, back_attended, attended, logs)


def feed_forward_kernel(normed_ref, middle_ref, up_ref, down_ref, active_ref, slope_ref, out_ref):
    @pl.when(pl.program_id(0) == 0)
    def _():
        out_ref[...] = middle_ref[...]

    active, slope = gelu_and_slope(dot_nn(normed_ref[...], up_ref[...]))
    active = active.astype(BF16)
    active_ref[...] = active
    slope_ref[...] = slope.astype(BF16)
    out_ref[...] += dot_nn(active, down_ref[...])


def feed_forward(normed, middle, matrix_up, matrix_down):
    tokens, width = normed.shape
    hidden = matrix_up.shape[1]
    tile = 512
    whole = pl.BlockSpec((tokens, width), lambda j: (0, 0))
    part = pl.BlockSpec((tokens, tile), lambda j: (0, j))
    return pl.pallas_call(
        feed_forward_kernel,
        grid=(hidden // tile,),
        in_specs=[whole, whole, pl.BlockSpec((width, tile), lambda j: (0, j)),
                  pl.BlockSpec((tile, width), lambda j: (j, 0))],
        out_specs=[part, part, whole],
        out_shape=[
            jax.ShapeDtypeStruct((tokens, hidden), BF16),
            jax.ShapeDtypeStruct((tokens, hidden), BF16),
            jax.ShapeDtypeStruct((tokens, width), F32),
        ],
        compiler_params=pltpu.CompilerParams(vmem_limit_bytes=VMEM_BYTES),
        cost_estimate=pl.CostEstimate(flops=9_600_000_000, bytes_accessed=20_000_000, transcendentals=3_000_000),
        name="feed_forward",
    )(normed, middle, matrix_up, matrix_down)


def feed_back_kernel(back_ref, slope_ref, up_ref, down_ref, back_up_ref, back_normed_ref):
    back_up = (dot_nt(back_ref[...], down_ref[...]) * slope_ref[...].astype(F32)).astype(BF16)
    back_up_ref[0] = back_up

    @pl.when(pl.program_id(0) == 0)
    def _():
        back_normed_ref[...] = jnp.zeros_like(back_normed_ref)

    back_normed_ref[...] += dot_nt(back_up, up_ref[...])


def feed_back(back_out, slope, matrix_up, matrix_down):
    tokens, width = back_out.shape
    hidden = matrix_up.shape[1]
    tile = 512
    half = hidden // tile // 2
    whole = pl.BlockSpec((tokens, width), lambda j: (0, 0))
    return pl.pallas_call(
        feed_back_kernel,
        grid=(hidden // tile,),
        in_specs=[whole, pl.BlockSpec((tokens, tile), lambda j: (0, j)),
                  pl.BlockSpec((width, tile), lambda j: (0, j)),
                  pl.BlockSpec((tile, width), lambda j: (j, 0))],
        out_specs=[pl.BlockSpec((1, tokens, tile), lambda j: (j // half, 0, j % half)), whole],
        out_shape=[
            jax.ShapeDtypeStruct((2, tokens, hidden // 2), BF16),
            jax.ShapeDtypeStruct((tokens, width), F32),
        ],
        compiler_params=pltpu.CompilerParams(vmem_limit_bytes=VMEM_BYTES),
        cost_estimate=pl.CostEstimate(flops=9_600_000_000, bytes_accessed=20_000_000, transcendentals=0),
        name="feed_back",
    )(back_out, slope, matrix_up, matrix_down)


def grad_up_kernel(chips, meta, ao, ax, bo, bx, keep, send, acc):
    rows = keep.shape[1]
    acc[...] = (dot_tn(ao[...], bo[0]) + dot_tn(ax[...], bx[...])).astype(BF16)
    for position in range(chips):
        chunk = acc[pl.ds(pl.multiple_of(meta[2 + position] * rows, 16), rows), :]
        if position < chips // 2:
            keep[position] = chunk
        else:
            send[position - chips // 2] = chunk


def grad_down_kernel(chips, meta, ao, ax, bo, bx, keep_in, send_in, keep, send):
    rows = keep.shape[1]
    each = ao.shape[1] // rows
    total = (dot_tn(ao[...], bo[...]) + dot_tn(ax[...], bx[...])).astype(BF16)
    for local in range(each):
        position = meta[2 + chips + pl.program_id(0) * each + local]
        chunk = total[local * rows : (local + 1) * rows]

        @pl.when(position < chips // 2)
        def _():
            keep[position] = chunk

        @pl.when(position >= chips // 2)
        def _():
            send[position - chips // 2] = chunk


def grad_branch_kernel(chips, meta, ho, hx, po, px, ao, ax, bo, bx, keep, send, acc):
    rows = keep.shape[1]
    step = pl.program_id(0)

    @pl.when(step < 3)
    def _():
        acc[...] = (dot_tn(ho[...], po[...]) + dot_tn(hx[...], px[...])).astype(BF16)

    @pl.when(step == 3)
    def _():
        acc[...] = (dot_tn(ao[...], bo[...]) + dot_tn(ax[...], bx[...])).astype(BF16)

    for position in range(chips):
        chunk = acc[pl.ds(pl.multiple_of(meta[2 + position] * rows, 16), rows), :]
        if position < chips // 2:
            keep[position] = chunk
        else:
            send[position - chips // 2] = chunk


def ordered(total, ids, chips):
    split = total.astype(BF16).reshape(chips, total.shape[0] // chips, total.shape[1])
    return jnp.take(split, ids, axis=0)


def mlp_gradients(meta, chips, core, normed, normed_x, back_up, back_up_x, active, active_x, back_out, back_out_x):
    tokens, width = normed.shape
    hidden = active.shape[1]
    half = width // 2
    rows = width // chips
    params = pltpu.CompilerParams(vmem_limit_bytes=VMEM_BYTES)
    if rows % 16 != 0:
        ids = meta[2 : 2 + chips]
        up = dot_tn(normed, lax.dynamic_index_in_dim(back_up, core, 0, False)) + dot_tn(normed_x, back_up_x)
        down = dot_tn(active, lax.dynamic_slice_in_dim(back_out, core * half, half, 1)) + dot_tn(active_x, back_out_x)
        up = ordered(up, ids, chips).reshape(chips, rows, 4, half)
        up = up.transpose(0, 2, 1, 3).reshape(chips, 4 * rows, half)
        both = jnp.concatenate([up, ordered(down, ids, chips)], -1)
        return both[: chips // 2], both[chips // 2 :]
    shape = jax.ShapeDtypeStruct((chips // 2, 4 * rows, 2 * half), BF16)
    whole = pl.BlockSpec((tokens, width), lambda j, m: (0, 0))
    keep, send = pl.pallas_call(
        functools.partial(grad_up_kernel, chips),
        grid_spec=pltpu.PrefetchScalarGridSpec(
            num_scalar_prefetch=1,
            grid=(4,),
            in_specs=[whole, whole, pl.BlockSpec((1, tokens, half), lambda j, m: (m[1], 0, j)),
                      pl.BlockSpec((tokens, half), lambda j, m: (0, j))],
            out_specs=[pl.BlockSpec((chips // 2, rows, half), lambda j, m: (0, j, 0))] * 2,
            scratch_shapes=[pltpu.VMEM((width, half), BF16)],
        ),
        out_shape=[shape, shape],
        compiler_params=params,
        cost_estimate=pl.CostEstimate(flops=4_800_000_000, bytes_accessed=7_000_000, transcendentals=0),
        name="gradient_up",
    )(meta, normed, normed_x, back_up, back_up_x)
    steps = hidden // width
    tile = pl.BlockSpec((tokens, width), lambda j, m: (0, j))
    out = pl.BlockSpec((chips // 2, 4 * rows, half), lambda j, m: (0, 0, 1))
    return pl.pallas_call(
        functools.partial(grad_down_kernel, chips),
        grid_spec=pltpu.PrefetchScalarGridSpec(
            num_scalar_prefetch=1,
            grid=(steps,),
            in_specs=[tile, tile, pl.BlockSpec((tokens, half), lambda j, m: (0, m[1])),
                      pl.BlockSpec((tokens, half), lambda j, m: (0, 0)),
                      pl.BlockSpec(memory_space=pl.ANY), pl.BlockSpec(memory_space=pl.ANY)],
            out_specs=[out, out],
        ),
        out_shape=[shape, shape],
        input_output_aliases={5: 0, 6: 1},
        compiler_params=params,
        cost_estimate=pl.CostEstimate(flops=4_800_000_000, bytes_accessed=10_000_000, transcendentals=0),
        name="gradient_down",
    )(meta, active, active_x, back_out, back_out_x, keep, send)


def branch_gradients(meta, chips, core, hidden, hidden_x, back_projected, back_projected_x, attended, attended_x, back_branch, back_branch_x):
    tokens, width = hidden.shape
    half = width // 2
    rows = width // chips
    if rows % 16 != 0:
        ids = meta[2 : 2 + chips]
        own = lax.dynamic_slice_in_dim(back_projected, core * 3 * half, 3 * half, 1)
        qkv = dot_tn(hidden, own) + dot_tn(hidden_x, back_projected_x)
        own = lax.dynamic_slice_in_dim(back_branch, core * half, half, 1)
        out = dot_tn(attended, own) + dot_tn(attended_x, back_branch_x)
        both = ordered(jnp.concatenate([qkv, out], -1), ids, chips)
        return both[: chips // 2], both[chips // 2 :]
    shape = jax.ShapeDtypeStruct((chips // 2, rows, 4 * half), BF16)
    whole = pl.BlockSpec((tokens, width), lambda j, m: (0, 0))
    return pl.pallas_call(
        functools.partial(grad_branch_kernel, chips),
        grid_spec=pltpu.PrefetchScalarGridSpec(
            num_scalar_prefetch=1,
            grid=(4,),
            in_specs=[
                whole, whole,
                pl.BlockSpec((tokens, half), lambda j, m: (0, 3 * m[1] + jnp.minimum(j, 2))),
                pl.BlockSpec((tokens, half), lambda j, m: (0, jnp.minimum(j, 2))),
                whole, whole,
                pl.BlockSpec((tokens, half), lambda j, m: (0, m[1])),
                pl.BlockSpec((tokens, half), lambda j, m: (0, 0)),
            ],
            out_specs=[pl.BlockSpec((chips // 2, rows, half), lambda j, m: (0, 0, j))] * 2,
            scratch_shapes=[pltpu.VMEM((width, half), BF16)],
        ),
        out_shape=[shape, shape],
        compiler_params=pltpu.CompilerParams(vmem_limit_bytes=VMEM_BYTES),
        cost_estimate=pl.CostEstimate(flops=4_800_000_000, bytes_accessed=8_000_000, transcendentals=0),
        name="gradient_branch",
    )(meta, hidden, hidden_x, back_projected, back_projected_x, attended, attended_x, back_branch, back_branch_x)


class Exchange:
    def __init__(self, dp):
        self.dp = dp
        self.chips = 2 * dp
        self.bits = int(math.log2(self.chips))
        self.core_pairs = [(s, s ^ 1) for s in range(4)]
        self.mirror_pairs = [(s, 3 - s) for s in range(4)]
        rest = list(range(2, self.bits))
        self.orders = ([1, 0] + rest, [0, 1] + rest)

    def swap_core(self, value):
        return lax.ppermute(value, "seq", self.core_pairs)

    def mirror(self, value):
        return lax.ppermute(value, "seq", self.mirror_pairs)

    def pairs(self, phase):
        result = []
        for device in range(2 * self.chips):
            chip = (device // 4) * 2 + (device % 4) // 2
            core = device % 2
            other = chip ^ (1 << self.orders[core][phase])
            result.append((device, (other // 2) * 4 + (other % 2) * 2 + core))
        return result

    def tables(self, chip, core):
        index = np.arange(self.chips)
        maps, inverses = [], []
        for order in self.orders:
            value = np.zeros_like(index)
            for phase, bit in enumerate(order):
                value |= ((index >> (self.bits - 1 - phase)) & 1) << bit
            inverse = np.zeros_like(index)
            inverse[value] = index
            maps.append(value.astype(np.int32))
            inverses.append(order)
        ids = chip ^ jnp.where(core == 0, jnp.asarray(maps[0]), jnp.asarray(maps[1]))
        relative = jnp.asarray(index.astype(np.int32)) ^ chip
        places = []
        for order in self.orders:
            place = jnp.zeros_like(relative)
            for phase, bit in enumerate(order):
                place = place | (((relative >> bit) & 1) << (self.bits - 1 - phase))
            places.append(place)
        return ids.astype(jnp.int32), jnp.where(core == 0, places[0], places[1]).astype(jnp.int32)

    def reduce_scatter(self, keep, send, kind):
        parts = [keep]
        for phase in range(self.bits):
            parts.append(lax.ppermute(send, AXES, self.pairs(phase)))
            size = parts[-1].shape[0]
            if phase < self.bits - 1:
                send = sum(part[size // 2 : size].astype(F32) for part in parts).astype(kind)
        return sum(part[0].astype(F32) for part in parts)


def halves(value, core, half):
    return lax.dynamic_slice_in_dim(value, (1 - core) * half, half, 1)


def by_core(core, mine, theirs, axis):
    return jnp.where(
        core == 0,
        jnp.concatenate([mine, theirs], axis),
        jnp.concatenate([theirs, mine], axis),
    )


def layer_forward(stream, weights, flag, exchange):
    gain_a, shift_a, matrix_qkv, matrix_out, gain_b, shift_b, matrix_up, matrix_down = weights
    width = stream.shape[-1]
    hidden = norm_rows(stream, gain_a, shift_a).astype(BF16)
    projected = dot_nn(hidden, matrix_qkv).astype(BF16)
    other = exchange.swap_core(projected[:, width:])
    attended, logs = attention_forward(flag, projected, other)
    middle = stream + dot_nn(attended, matrix_out)
    normed = norm_rows(middle, gain_b, shift_b).astype(BF16)
    active, slope, output = feed_forward(normed, middle, matrix_up, matrix_down)
    remote = tuple(exchange.swap_core(v) for v in (hidden, attended, normed, active))
    kept = (stream, hidden, projected, other, logs, attended, middle, normed, active, slope, remote)
    return output, kept


def layer_backward(upstream, weights, kept, flag, meta, core, exchange):
    gain_a, shift_a, matrix_qkv, matrix_out, gain_b, shift_b, matrix_up, matrix_down = weights
    stream, hidden, projected, other, logs, attended, middle, normed, active, slope, remote = kept
    hidden_x, attended_x, normed_x, active_x = remote
    width = stream.shape[-1]
    chips = exchange.chips
    half = width // 2
    back_out = upstream.astype(BF16)
    back_up, back_normed = feed_back(back_out, slope, matrix_up, matrix_down)
    back_out_x = exchange.swap_core(halves(back_out, core, half))
    back_up_x = exchange.swap_core(lax.dynamic_index_in_dim(back_up, 1 - core, 0, False))
    keep, send = mlp_gradients(
        meta, chips, core, normed, normed_x, back_up, back_up_x, active, active_x, back_out, back_out_x
    )
    mlp_share = exchange.reduce_scatter(keep, send, BF16)
    unused, norm_pull_two = jax.vjp(norm_rows, middle, gain_b, shift_b)
    back_middle, grad_gain_b, grad_shift_b = norm_pull_two(back_normed)
    back_middle = back_middle + upstream
    back_branch = back_middle.astype(BF16)
    back_branch_x = exchange.swap_core(halves(back_branch, core, half))
    back_attended = dot_nt(back_branch, matrix_out).astype(BF16)
    back_q, back_k, back_v, back_kx, back_vx = attention_backward(
        flag, projected, other, back_attended, attended, logs
    )
    back_k = back_k + exchange.swap_core(back_kx).astype(F32)
    back_v = back_v + exchange.swap_core(back_vx).astype(F32)
    back_projected = jnp.concatenate([back_q, back_k.astype(BF16), back_v.astype(BF16)], -1)
    back_projected_x = exchange.swap_core(halves(back_projected, core, 3 * half))
    keep, send = branch_gradients(
        meta, chips, core, hidden, hidden_x, back_projected, back_projected_x,
        attended, attended_x, back_branch, back_branch_x,
    )
    branch_share = exchange.reduce_scatter(keep, send, BF16)
    back_hidden = dot_nt(back_projected, matrix_qkv)
    unused, norm_pull_one = jax.vjp(norm_rows, stream, gain_a, shift_a)
    back_stream, grad_gain_a, grad_shift_a = norm_pull_one(back_hidden)
    rows = jnp.stack([grad_gain_a, grad_shift_a, grad_gain_b, grad_shift_b])
    return back_stream + back_middle, rows, mlp_share, branch_share


def unpack_mlp(share, core, exchange):
    long, wide = share.shape
    rows, half, each = long // 4, wide // 2, long // 8
    up = share[:, :half].reshape(4, 2, each, half)
    down = share[:, half:].reshape(2, 4 * each, half)

    def pick(which):
        return jnp.concatenate(
            [lax.dynamic_index_in_dim(up, which, 1, False).reshape(4 * each, half),
             lax.dynamic_index_in_dim(down, which, 0, False)], -1)

    mine, theirs = pick(core), exchange.swap_core(pick(1 - core))

    def widen(value):
        return value[:, :half].reshape(4, each, half).transpose(1, 0, 2).reshape(each, 4 * half)

    grad_up = by_core(core, widen(mine), widen(theirs), 1)
    grad_down = by_core(core, mine[:, half:], theirs[:, half:], 1)
    return grad_up, grad_down


def unpack_branch(share, core, exchange):
    rows, wide = share.shape
    each, half = rows // 2, wide // 4
    split = share.reshape(2, each, wide)
    mine = lax.dynamic_index_in_dim(split, core, 0, False)
    theirs = exchange.swap_core(lax.dynamic_index_in_dim(split, 1 - core, 0, False))
    grad_qkv = by_core(core, mine[:, : 3 * half], theirs[:, : 3 * half], 1)
    grad_out = by_core(core, mine[:, 3 * half :], theirs[:, 3 * half :], 1)
    return grad_qkv, grad_out


def per_device(
    inputs, cotangent, task_table, type_counts,
    gain_one, bias_one, proj_qkv, proj_out, gain_two, bias_two, proj_up, proj_down,
):
    slots, rows, width = inputs.shape
    length = rows * lax.axis_size("seq")
    exchange = Exchange(lax.axis_size("dp"))
    place = lax.axis_index("seq")
    side, core = place // 2, place % 2
    chip = lax.axis_index("dp") * 2 + side
    low = jnp.minimum(place, 3 - place)
    own_first = place < 2
    ids, places = exchange.tables(chip, core)
    flag = low.astype(jnp.int32).reshape(1)
    meta = jnp.concatenate([flag, core.astype(jnp.int32).reshape(1), ids, places])

    def gather_slot(value):
        own = lax.dynamic_index_in_dim(value, side, 0, False)
        got = exchange.mirror(lax.dynamic_index_in_dim(value, 1 - side, 0, False))
        return jnp.where(own_first, jnp.concatenate([own, got]), jnp.concatenate([got, own]))

    def return_slot(value):
        first, second = value[:rows], value[rows:]
        own = jnp.where(own_first, first, second)
        got = exchange.mirror(jnp.where(own_first, second, first))
        return jnp.where(side == 0, jnp.stack([own, got]), jnp.stack([got, own]))

    stream = gather_slot(inputs).astype(F32)
    cotangent = gather_slot(cotangent)
    choose = (task_table[:, None] == jnp.arange(TASKS, dtype=jnp.int32)[None, :]).astype(F32)
    targets = (length - type_counts[:, 0]).astype(F32)
    totals = lax.psum(jnp.sum(choose * targets[:, None], 0), "dp")
    factor = jnp.sum(totals) / TASKS / totals
    seq_weight = jnp.sum(choose * factor[None, :], 1)
    own_weight = lax.dynamic_index_in_dim(seq_weight, side, 0, False)
    own_start = lax.dynamic_index_in_dim(type_counts[:, 0], side, 0, False)
    steps = jnp.arange(rows, dtype=jnp.int32)
    query_pos = jnp.concatenate([low * rows + steps, (3 - low) * rows + steps])
    scale = jnp.where(query_pos >= own_start, own_weight, 0.0)
    upstream = cotangent.astype(F32) * scale[:, None]

    stacked = (gain_one, bias_one, proj_qkv, proj_out, gain_two, bias_two, proj_up, proj_down)
    kept_all = []
    for section in range(LAYERS):
        weights = tuple(weight[section] for weight in stacked)
        stream, kept = layer_forward(stream, weights, flag, exchange)
        kept_all.append(kept)
    outputs = return_slot(stream.astype(BF16))
    small, mlp, branch = [None] * LAYERS, [None] * LAYERS, [None] * LAYERS
    for section in reversed(range(LAYERS)):
        weights = tuple(weight[section] for weight in stacked)
        upstream, small[section], mlp[section], branch[section] = layer_backward(
            upstream, weights, kept_all[section], flag, meta, core, exchange
        )
    back_inputs = return_slot(upstream.astype(BF16)).astype(F32)

    chips = exchange.chips
    each = width // chips // 2
    table = jnp.concatenate(small).reshape(8, chips, 2, each).transpose(1, 2, 0, 3)
    mine = lax.dynamic_index_in_dim(table, core, 1, False)
    theirs = exchange.swap_core(lax.dynamic_index_in_dim(table, 1 - core, 1, False))
    table = jnp.take(mine + theirs, ids, axis=0)
    table = exchange.reduce_scatter(table[: chips // 2], table[chips // 2 :], F32)
    table = table.reshape(LAYERS, 4, each)
    ups, downs = zip(*(unpack_mlp(share, core, exchange) for share in mlp))
    qkvs, outs = zip(*(unpack_branch(share, core, exchange) for share in branch))
    return (
        outputs, back_inputs, table[:, 0], table[:, 1], jnp.stack(qkvs), jnp.stack(outs),
        table[:, 2], table[:, 3], jnp.stack(ups), jnp.stack(downs),
    )


def solution(mesh):
    tokens = P("dp", "seq", None)
    shared = P(None, AXES)
    in_specs = (tokens, tokens, P("dp"), P("dp", None)) + (P(),) * 8
    out_specs = (
        tokens, tokens, shared, shared, P(None, AXES, None), P(None, AXES, None),
        shared, shared, P(None, AXES, None), P(None, AXES, None),
    )
    return jax.shard_map(
        per_device, mesh=mesh, in_specs=in_specs, out_specs=out_specs, check_vma=False
    )
```

time: 1240 us -> 515 us (0.42)
  waiting for transfers between devices: 731 us -> 118 us
  matrix products: 258 us -> 25.9 us
  Pallas kernels: 0 us -> 177 us
  other arithmetic: 130 us -> 56.9 us
  blocking collectives: 61.7 us -> 21.8 us
  local copies, waits for them, and re-layouts: 40.7 us -> 73.3 us
  starting transfers between devices: 0.67 us -> 31.6 us
  between operations: 16.4 us -> 3.22 us
    reduce_scatter x8 -> x0, waiting for transfers between devices: 685 us -> none  [the longest x4 627 us: per_device(): lax.psum_scatter(summed, ('dp', 'seq'), scatter_dimension=1, tiled=True)]
    dot_general x36 -> x8, matrix products: 258 us -> 25.9 us  [the longest x4 13.3 us: dot_nt(): lax.dot_general(a, b, (((1,), (1,)), ((), ())), preferred_element_type=F32)]
    pallas_call x0 -> x14, Pallas kernels: none -> 177 us  [the longest x2 45.7 us: attention_backward(): pl.pallas_call(attention_backward_kernel, grid_spec=pltpu.PrefetchScalarG...]
    ppermute x0 -> x51, waiting for transfers between devices: none -> 118 us  [the longest x20 95.2 us: reduce_scatter(): parts.append(lax.ppermute(send, AXES, self.pairs(phase)))]
    all_gather x4 -> x0, waiting for transfers between devices: 45.9 us -> none  [the longest x2 33.8 us: layer_forward(): lax.all_gather(local_keys, 'seq', axis=1, tiled=True)]
    convert_element_type x7 -> x28, other arithmetic: 65.5 us -> 23.4 us  [the longest x12 7.62 us: reduce_scatter(): sum((part[size // 2:size].astype(F32) for part in parts)).astype(kind)]
    unnamed x1 -> x0, blocking collectives: 40 us -> none
    ppermute x0 -> x51, starting transfers between devices: none -> 31.6 us  [the longest x20 18 us: reduce_scatter(): parts.append(lax.ppermute(send, AXES, self.pairs(phase)))]
  transfers between devices with their start and end apart: 12 -> 51, of which waited for: 11 -> 20; matrix products, arithmetic and copies ran while one was open for 15% -> 26% of each run, Pallas kernels for 0% -> 22%
where the time goes in v1:
time: 515 us; the launch traced here: 509 us
  Pallas kernels  177 us (34%)
  waiting for transfers between devices  118 us (23%)
  local copies, waits for them, and re-layouts  73.3 us (14%)
  other arithmetic  56.9 us (11%)
  starting transfers between devices  31.6 us (6%)
  matrix products  25.9 us (5%)
  blocking collectives  21.8 us (4%)
    ppermute x20, waiting for transfers between devices, reduce_scatter(): parts.append(lax.ppermute(send, AXES, self.pairs(phase)))  95.2 us
    pallas_call x2, Pallas kernels, attention_backward(): pl.pallas_call(attention_backward_kernel, grid_spec=pltpu.PrefetchScalarG...  45.7 us
    pallas_call x2, Pallas kernels, feed_forward(): pl.pallas_call(feed_forward_kernel, grid=(hidden // tile,), in_specs=[who...  29.2 us
    pallas_call x2, Pallas kernels, attention_forward(): pl.pallas_call(attention_forward_kernel, grid_spec=pltpu.PrefetchScalarGr...  26.5 us
    pallas_call x2, Pallas kernels, feed_back(): pl.pallas_call(feed_back_kernel, grid=(hidden // tile,), in_specs=[whole,...  25.2 us
    concatenate x17, local copies, waits for them, and re-layouts, per_device(): jnp.concatenate(small).reshape(8, chips, 2, each).transpose(1, 2, 0, 3)  22.1 us
    psum x1, blocking collectives, per_device(): totals = lax.psum(jnp.sum(choose * targets[:, None], 0), 'dp')  21.8 us
    ppermute x4, waiting for transfers between devices, mirror(): return lax.ppermute(value, 'seq', self.mirror_pairs)  18.5 us
  transfers between devices with their start and end apart: 51, of which 20 were waited for; matrix products, arithmetic and copies ran while one was open for 26% of the time, Pallas kernels for 22%

profile of v1, /device:TPU:0, one launch (start us, length us, event | category | flops | bytes accessed | tf_op | source)
XLA Modules:
  0.0 508.5 jit_solution(7523610573977952123)
XLA Ops:
  2.0 2.5 collective-permute-start
  4.9 9.0 %collective-permute-done = bf16[256,768]{1,0:T(8,128)(2,1)S(1)} collective-permute-done((bf16[256,768]{1,0:T(8,128)(2,1)S(1)}, bf16[256,768]{1,0:T(8,128)(2,1)S(1)}, u32[]{:S(2)}, u32[]{:S(2)}) %collective-permute-start) | collective-permute-done | bytes 393248 | tf_op jit(solution)/shard_map/ppermute | solution.py:463
  15.1 4.3 convolution_convert_fusion.1.q_ref.ko_ref.vo_ref
  22.5 8.2 %slice_bitcast_fusion.1 = (bf16[768,3072]{1,0:T(8,128)(2,1)}, bf16[768,3072]{1,0:T(8,128)(2,1)}) fusion(bf16[2,768,3072]{2,1,0:T(8,128)(2,1)} %param.25), kind=kLoop, calls=%fused_computation.2 | loop fusion | bytes 18874368 | tf_op jit(solution)/shard_map/squeeze | solution.py:648
  30.8 21.8 %psum.7 = f32[3]{0:T(128)S(1)} all-reduce(f32[3]{0:T(128)S(1)} %select_reduce_fusion.1), channel_id=1, replica_groups=mesh['dp'=8,'seq'=4] {'dp'}, use_global_device_ids=true, to_apply=%region_9.10 | all-reduce | flops 3 | bytes 24 | tf_op jit(solution)/shard_map/psum | solution.py:635
  53.9 8.0 %slice_bitcast_fusion = (bf16[3072,768]{1,0:T(8,128)(2,1)}, bf16[3072,768]{1,0:T(8,128)(2,1)}) fusion(bf16[2,3072,768]{2,1,0:T(8,128)(2,1)} %param.26), kind=kLoop, calls=%fused_computation.1 | loop fusion | bytes 18874368 | tf_op jit(solution)/shard_map/squeeze | solution.py:648
  61.9 13.2 %attention_forward.2 = (bf16[512,768]{1,0:T(8,128)(2,1)}, f32[6,8,512]{2,1,0:T(8,128)}) custom-call(s32[1]{0:T(128)} %bitcast.2.meta, bf16[512,2304]{1,0:T(8,128)(2,1)} %copy-done.38, bf16[512,2304]{1,0:T(8,128)(2,1)} %copy-done.38, bf16[512,2304]{1,0:T(8,128)(2,1)} %copy-done.38, bf16[512,1536]{1,0:T(8,128)(2,1)} %collective-permute-done.1.kx_ref.vx_ref, ...), custom_call_target="tpu_custom_call" | custom-call | flops 8000000000 | bytes 4000000 | tf_op jit(solution)/shard_map/attention_forward/pallas_call | solution.py:122
  75.1 2.0 fusion.50
  78.7 14.6 %feed_forward.2 = (bf16[512,3072]{1,0:T(8,128)(2,1)}, bf16[512,3072]{1,0:T(8,128)(2,1)}, f32[512,768]{1,0:T(8,128)}) custom-call(bf16[512,768]{1,0:T(8,128)(2,1)} %add_convert_fusion.9.normed_ref.ao, f32[512,768]{1,0:T(8,128)} %copy-done.3, bf16[768,3072]{1,0:T(8,128)(2,1)} %get-tuple-element.116.up_ref, bf16[3072,768]{1,0:T(8,128)(2,1)} %get-tuple-element.114.down_ref), custom_call_target="tpu_custom_call" | custom-call | flops 9600000000 | bytes 20000000 | tf_op jit(solution)/shard_map/feed_forward/pallas_call | solution.py:256
  96.7 4.2 convolution_convert_fusion.q_ref.ko_ref.vo_ref
  108.4 13.4 %attention_forward.3 = (bf16[512,768]{1,0:T(8,128)(2,1)}, f32[6,8,512]{2,1,0:T(8,128)}) custom-call(s32[1]{0:T(128)} %bitcast.2.meta, bf16[512,2304]{1,0:T(8,128)(2,1)} %copy-done.39, bf16[512,2304]{1,0:T(8,128)(2,1)} %copy-done.39, bf16[512,2304]{1,0:T(8,128)(2,1)} %copy-done.39, bf16[512,1536]{1,0:T(8,128)(2,1)} %collective-permute-done.2.kx_ref.vx_ref, ...), custom_call_target="tpu_custom_call" | custom-call | flops 8000000000 | bytes 4000000 | tf_op jit(solution)/shard_map/attention_forward/pallas_call | solution.py:122
  121.8 2.0 fusion.51
  125.4 14.6 %feed_forward.3 = (bf16[512,3072]{1,0:T(8,128)(2,1)}, bf16[512,3072]{1,0:T(8,128)(2,1)}, f32[512,768]{1,0:T(8,128)}) custom-call(bf16[512,768]{1,0:T(8,128)(2,1)} %add_convert_fusion.7.normed_ref.ao, f32[512,768]{1,0:T(8,128)} %copy-done.1, bf16[768,3072]{1,0:T(8,128)(2,1)} %get-tuple-element.115.up_ref, bf16[3072,768]{1,0:T(8,128)(2,1)} %get-tuple-element.113.down_ref), custom_call_target="tpu_custom_call" | custom-call | flops 9600000000 | bytes 20000000 | tf_op jit(solution)/shard_map/feed_forward/pallas_call | solution.py:256
  140.0 12.5 %feed_back.2 = (bf16[2,512,1536]{2,1,0:T(8,128)(2,1)}, f32[512,768]{1,0:T(8,128)}) custom-call(bf16[512,768]{1,0:T(8,128)(2,1)} %fusion.21.back_ref.bo, bf16[512,3072]{1,0:T(8,128)(2,1)} %get-tuple-element.50.slope_ref, bf16[768,3072]{1,0:T(8,128)(2,1)} %get-tuple-element.115.up_ref, bf16[3072,768]{1,0:T(8,128)(2,1)} %get-tuple-element.113.down_ref), custom_call_target="tpu_custom_call" | custom-call | flops 9600000000 | bytes 20000000 | tf_op jit(solution)/shard_map/feed_back/pallas_call | solution.py:290
  152.5 2.7 multiply_reduce_fusion
  159.7 23.2 %attention_backward.2 = (bf16[512,768]{1,0:T(8,128)(2,1)}, f32[512,768]{1,0:T(8,128)}, f32[512,768]{1,0:T(8,128)}, bf16[512,768]{1,0:T(8,128)(2,1)}, bf16[512,768]{1,0:T(8,128)(2,1)}) custom-call(s32[1]{0:T(128)} %bitcast.2.meta, bf16[512,2304]{1,0:T(8,128)(2,1)} %copy-done.39, bf16[512,2304]{1,0:T(8,128)(2,1)} %copy-done.39, bf16[512,2304]{1,0:T(8,128)(2,1)} %copy-done.39, ...), custom_call_target="tpu_custom_call" | custom-call | flops 16000000000 | bytes 9000000 | tf_op jit(solution)/shard_map/attention_backward/pallas_call | solution.py:216
  192.9 2.7 dynamic-slice_bitcast_fusion
  196.9 2.1 maximum_select_fusion.1
  202.1 4.9 multiply_reduce_fusion.1
  211.1 12.7 %feed_back.3 = (bf16[2,512,1536]{2,1,0:T(8,128)(2,1)}, f32[512,768]{1,0:T(8,128)}) custom-call(bf16[512,768]{1,0:T(8,128)(2,1)} %get-tuple-element.107.back_ref.bo, bf16[512,3072]{1,0:T(8,128)(2,1)} %get-tuple-element.58.slope_ref, bf16[768,3072]{1,0:T(8,128)(2,1)} %get-tuple-element.116.up_ref, bf16[3072,768]{1,0:T(8,128)(2,1)} %get-tuple-element.114.down_ref), custom_call_target="tpu_custom_call" | custom-call | flops 9600000000 | bytes 20000000 | tf_op jit(solution)/shard_map/feed_back/pallas_call | solution.py:290
  223.8 2.7 multiply_reduce_fusion.2
  230.6 22.5 %attention_backward.3 = (bf16[512,768]{1,0:T(8,128)(2,1)}, f32[512,768]{1,0:T(8,128)}, f32[512,768]{1,0:T(8,128)}, bf16[512,768]{1,0:T(8,128)(2,1)}, bf16[512,768]{1,0:T(8,128)(2,1)}) custom-call(s32[1]{0:T(128)} %bitcast.2.meta, bf16[512,2304]{1,0:T(8,128)(2,1)} %copy-done.38, bf16[512,2304]{1,0:T(8,128)(2,1)} %copy-done.38, bf16[512,2304]{1,0:T(8,128)(2,1)} %copy-done.38, ...), custom_call_target="tpu_custom_call" | custom-call | flops 16000000000 | bytes 9000000 | tf_op jit(solution)/shard_map/attention_backward/pallas_call | solution.py:216
  268.1 2.8 dynamic-slice_bitcast_fusion.1
  276.0 5.0 fusion.41
  291.1 8.1 %gradient_up.3 = (bf16[8,192,768]{2,1,0:T(8,128)(2,1)}, bf16[8,192,768]{2,1,0:T(8,128)(2,1)}) custom-call(s32[34]{0:T(128)} %pad_add_fusion.meta, bf16[512,768]{1,0:T(8,128)(2,1)} %add_convert_fusion.7.normed_ref.ao, bf16[512,768]{1,0:T(8,128)(2,1)} %collective-permute-done.44.ax, bf16[2,512,1536]{2,1,0:T(8,128)(2,1)} %get-tuple-element.77.bo, ...), custom_call_target="tpu_custom_call" | custom-call | flops 4800000000 | bytes 7000000 | tf_op jit(solution)/shard_map/gradient_up/pallas_call | solution.py:376
  299.8 2.1 gather_fusion
  303.1 1.9 pad_maximum_fusion.1.po
  305.0 2.0 collective-permute-done.11
  315.1 8.5 %gradient_branch.3 = (bf16[8,48,1536]{2,1,0:T(8,128)(2,1)}, bf16[8,48,1536]{2,1,0:T(8,128)(2,1)}) custom-call(s32[34]{0:T(128)} %pad_add_fusion.meta, bf16[512,768]{1,0:T(8,128)(2,1)} %add_convert_fusion.8.ho, bf16[512,768]{1,0:T(8,128)(2,1)} %collective-permute-done.24.hx, bf16[512,2304]{1,0:T(8,128)(2,1)} %pad_maximum_fusion.po, ...), custom_call_target="tpu_custom_call" | custom-call | flops 4800000000 | bytes 8000000 | tf_op jit(solution)/shard_map/gradient_branch/pallas_call | solution.py:426
  323.7 2.0 collective-permute-start.9
  326.5 8.6 %collective-permute-done.9 = bf16[256,768]{1,0:T(8,128)(2,1)S(1)} collective-permute-done((bf16[256,768]{1,0:T(8,128)(2,1)S(1)}, bf16[256,768]{1,0:T(8,128)(2,1)S(1)}, u32[]{:S(2)}, u32[]{:S(2)}) %collective-permute-start.9) | collective-permute-done | bytes 393248 | tf_op jit(solution)/shard_map/ppermute | solution.py:463
  337.8 8.0 %gradient_up.2 = (bf16[8,192,768]{2,1,0:T(8,128)(2,1)}, bf16[8,192,768]{2,1,0:T(8,128)(2,1)}) custom-call(s32[34]{0:T(128)} %pad_add_fusion.meta, bf16[512,768]{1,0:T(8,128)(2,1)} %add_convert_fusion.9.normed_ref.ao, bf16[512,768]{1,0:T(8,128)(2,1)} %copy-done.104, bf16[2,512,1536]{2,1,0:T(8,128)(2,1)} %get-tuple-element.71.bo, ...), custom_call_target="tpu_custom_call" | custom-call | flops 4800000000 | bytes 7000000 | tf_op jit(solution)/shard_map/gradient_up/pallas_call | solution.py:376
  351.2 8.7 %gradient_down.2 = (bf16[8,192,768]{2,1,0:T(8,128)(2,1)}, bf16[8,192,768]{2,1,0:T(8,128)(2,1)}) custom-call(s32[34]{0:T(128)} %pad_add_fusion.meta, bf16[512,3072]{1,0:T(8,128)(2,1)} %get-tuple-element.70.ao, bf16[512,3072]{1,0:T(8,128)(2,1)} %collective-permute-done.33.ax, ...), custom_call_target="tpu_custom_call", output_to_operand_aliasing={{0}: (5, {}), {1}: (6, {})} | custom-call | flops 4800000000 | bytes 10000000 | tf_op jit(solution)/shard_map/gradient_down/pallas_call | solution.py:394
  360.8 8.5 %gradient_branch.2 = (bf16[8,48,1536]{2,1,0:T(8,128)(2,1)}, bf16[8,48,1536]{2,1,0:T(8,128)(2,1)}) custom-call(s32[34]{0:T(128)} %pad_add_fusion.meta, bf16[512,768]{1,0:T(8,128)(2,1)} %copy-done.42, bf16[512,768]{1,0:T(8,128)(2,1)} %copy-done.105, bf16[512,2304]{1,0:T(8,128)(2,1)} %copy-done.16, bf16[512,1152]{1,0:T(8,128)(2,1)} %collective-permute-done.16.px, ...), custom_call_target="tpu_custom_call" | custom-call | flops 4800000000 | bytes 8000000 | tf_op jit(solution)/shard_map/gradient_branch/pallas_call | solution.py:426
  372.0 8.9 %gradient_down.3 = (bf16[8,192,768]{2,1,0:T(8,128)(2,1)}, bf16[8,192,768]{2,1,0:T(8,128)(2,1)}) custom-call(s32[34]{0:T(128)} %pad_add_fusion.meta, bf16[512,3072]{1,0:T(8,128)(2,1)} %get-tuple-element.76.ao, bf16[512,3072]{1,0:T(8,128)(2,1)} %collective-permute-done.42.ax, ...), custom_call_target="tpu_custom_call", output_to_operand_aliasing={{0}: (5, {}), {1}: (6, {})} | custom-call | flops 4800000000 | bytes 10000000 | tf_op jit(solution)/shard_map/gradient_down/pallas_call | solution.py:394
  382.7 3.0 collective-permute-start.31
  385.7 16.1 %collective-permute-done.19 = bf16[8,48,1536]{2,1,0:T(8,128)(2,1)S(1)} collective-permute-done((bf16[8,48,1536]{2,1,0:T(8,128)(2,1)}, bf16[8,48,1536]{2,1,0:T(8,128)(2,1)S(1)}, u32[]{:S(2)}, u32[]{:S(2)}) %collective-permute-start.19) | collective-permute-done | bytes 1179680 | tf_op jit(solution)/shard_map/ppermute | solution.py:498
  405.3 13.0 %collective-permute-done.20 = bf16[4,48,1536]{2,1,0:T(8,128)(2,1)S(1)} collective-permute-done((bf16[4,48,1536]{2,1,0:T(8,128)(2,1)S(1)}, bf16[4,48,1536]{2,1,0:T(8,128)(2,1)S(1)}, u32[]{:S(2)}, u32[]{:S(2)}) %collective-permute-start.20) | collective-permute-done | bytes 589856 | tf_op jit(solution)/shard_map/ppermute | solution.py:498
  419.8 7.3 %collective-permute-done.21 = bf16[2,48,1536]{2,1,0:T(8,128)(2,1)S(1)} collective-permute-done((bf16[2,48,1536]{2,1,0:T(8,128)(2,1)S(1)}, bf16[2,48,1536]{2,1,0:T(8,128)(2,1)S(1)}, u32[]{:S(2)}, u32[]{:S(2)}) %collective-permute-start.21) | collective-permute-done | bytes 294944 | tf_op jit(solution)/shard_map/ppermute | solution.py:498
  428.1 3.0 collective-permute-start.22
  431.9 3.9 collective-permute-done.22
  438.9 8.7 %collective-permute-done.38 = bf16[4,192,768]{2,1,0:T(8,128)(2,1)S(1)} collective-permute-done((bf16[4,192,768]{2,1,0:T(8,128)(2,1)S(1)}, bf16[4,192,768]{2,1,0:T(8,128)(2,1)S(1)}, u32[]{:S(2)}, u32[]{:S(2)}) %collective-permute-start.38) | collective-permute-done | bytes 1179680 | tf_op jit(solution)/shard_map/ppermute | solution.py:498
  449.1 12.7 %collective-permute-done.39 = bf16[2,192,768]{2,1,0:T(8,128)(2,1)S(1)} collective-permute-done((bf16[2,192,768]{2,1,0:T(8,128)(2,1)S(1)}, bf16[2,192,768]{2,1,0:T(8,128)(2,1)S(1)}, u32[]{:S(2)}, u32[]{:S(2)}) %collective-permute-start.39) | collective-permute-done | bytes 589856 | tf_op jit(solution)/shard_map/ppermute | solution.py:498
  461.9 3.0 collective-permute-start.40
  466.4 11.6 %collective-permute-done.40 = bf16[1,192,768]{2,1,0:T(8,128)(2,1)S(1)} collective-permute-done((bf16[1,192,768]{2,1,0:T(8,128)(2,1)S(1)}, bf16[1,192,768]{2,1,0:T(8,128)(2,1)S(1)}, u32[]{:S(2)}, u32[]{:S(2)}) %collective-permute-start.40) | collective-permute-done | bytes 294944 | tf_op jit(solution)/shard_map/ppermute | solution.py:498
  482.8 4.6 collective-permute-done.48
  487.4 1.9 add_convert_fusion.14
  491.4 11.8 %collective-permute-done.49 = bf16[1,192,768]{2,1,0:T(8,128)(2,1)S(1)} collective-permute-done((bf16[1,192,768]{2,1,0:T(8,128)(2,1)}, bf16[1,192,768]{2,1,0:T(8,128)(2,1)S(1)}, u32[]{:S(2)}, u32[]{:S(2)}) %collective-permute-start.49) | collective-permute-done | bytes 294944 | tf_op jit(solution)/shard_map/ppermute | solution.py:498
  (465 shorter events, 125.8 us)
Async XLA Ops:
  2.0 12.0 %collective-permute-start = (bf16[256,768]{1,0:T(8,128)(2,1)S(1)}, bf16[256,768]{1,0:T(8,128)(2,1)S(1)}, u32[]{:S(2)}, u32[]{:S(2)}) collective-permute-start(bf16[256,768]{1,0:T(8,128)(2,1)S(1)} %get-tuple-element.123), channel_id=1, source_target_pairs={{0,3},{1,2},{2,1},{3,0},{4,7},{5,6},{6,5},{7,4},{8,11},{9,10},{10,... | collective-permute-start | bytes 1179656 | tf_op jit(solution)/shard_map/ppermute | solution.py:463
  4.5 102.8 %collective-permute-start.4 = (bf16[256,768]{1,0:T(8,128)(2,1)S(1)}, bf16[256,768]{1,0:T(8,128)(2,1)S(1)}, u32[]{:S(2)}, u32[]{:S(2)}) collective-permute-start(bf16[256,768]{1,0:T(8,128)(2,1)S(1)} %get-tuple-element.119), channel_id=1, source_target_pairs={{0,3},{1,2},{2,1},{3,0},{4,7},{5,6},{6,5},{7,4},{8,11},{9,10},{10,... | collective-permute-start | bytes 1179656 | tf_op jit(solution)/shard_map/ppermute | solution.py:463
  21.4 40.5 %collective-permute-start.1 = (bf16[512,1536]{1,0:T(8,128)(2,1)}, bf16[512,1536]{1,0:T(8,128)(2,1)}, u32[]{:S(2)}, u32[]{:S(2)}) collective-permute-start(bf16[512,1536]{1,0:T(8,128)(2,1)} %slice.456), channel_id=1, source_target_pairs={{0,1},{1,0},{2,3},{3,2},{4,5},{5,4},{6,7},{7,6},{8,9},{9,8},{10,11... | collective-permute-start | bytes 4718600 | tf_op jit(solution)/shard_map/ppermute | solution.py:460
  102.9 5.5 %collective-permute-start.2 = (bf16[512,1536]{1,0:T(8,128)(2,1)}, bf16[512,1536]{1,0:T(8,128)(2,1)}, u32[]{:S(2)}, u32[]{:S(2)}) collective-permute-start(bf16[512,1536]{1,0:T(8,128)(2,1)} %slice.457), channel_id=1, source_target_pairs={{0,1},{1,0},{2,3},{3,2},{4,5},{5,4},{6,7},{7,6},{8,9},{9,8},{10,11... | collective-permute-start | bytes 4718600 | tf_op jit(solution)/shard_map/ppermute | solution.py:460
  182.9 16.1 %collective-permute-start.6 = (bf16[512,768]{1,0:T(8,128)(2,1)}, bf16[512,768]{1,0:T(8,128)(2,1)}, u32[]{:S(2)}, u32[]{:S(2)}) collective-permute-start(bf16[512,768]{1,0:T(8,128)(2,1)} %get-tuple-element.57), channel_id=1, source_target_pairs={{0,1},{1,0},{2,3},{3,2},{4,5},{5,4},{6,7},{7,6},{8,9},{9,8},{10,11... | collective-permute-start | bytes 2359304 | tf_op jit(solution)/shard_map/ppermute | solution.py:460
  183.8 126.9 %collective-permute-start.24 = (bf16[512,768]{1,0:T(8,128)(2,1)}, bf16[512,768]{1,0:T(8,128)(2,1)}, u32[]{:S(2)}, u32[]{:S(2)}) collective-permute-start(bf16[512,768]{1,0:T(8,128)(2,1)} %add_convert_fusion.8.ho), channel_id=1, source_target_pairs={{0,1},{1,0},{2,3},{3,2},{4,5},{5,4},{6,7},{7,6},{8,9},{9,8},{10,11... | collective-permute-start | bytes 2359304 | tf_op jit(solution)/shard_map/ppermute | solution.py:460
  184.3 165.2 %collective-permute-start.33 = (bf16[512,3072]{1,0:T(8,128)(2,1)}, bf16[512,3072]{1,0:T(8,128)(2,1)}, u32[]{:S(2)}, u32[]{:S(2)}) collective-permute-start(bf16[512,3072]{1,0:T(8,128)(2,1)} %get-tuple-element.70.ao), channel_id=1, source_target_pairs={{0,1},{1,0},{2,3},{3,2},{4,5},{5,4},{6,7},{7,6},{8,9},{9,8},{10,11... | collective-permute-start | bytes 9437192 | tf_op jit(solution)/shard_map/ppermute | solution.py:460
  185.3 11.1 %collective-permute-start.3 = (bf16[256,768]{1,0:T(8,128)(2,1)}, bf16[256,768]{1,0:T(8,128)(2,1)}, u32[]{:S(2)}, u32[]{:S(2)}) collective-permute-start(bf16[256,768]{1,0:T(8,128)(2,1)} %get-tuple-element.122), channel_id=1, source_target_pairs={{0,3},{1,2},{2,1},{3,0},{4,7},{5,6},{6,5},{7,4},{8,11},{9,10},{10,... | collective-permute-start | bytes 1179656 | tf_op jit(solution)/shard_map/ppermute | solution.py:463
  186.4 14.0 %collective-permute-start.5 = (bf16[512,768]{1,0:T(8,128)(2,1)}, bf16[512,768]{1,0:T(8,128)(2,1)}, u32[]{:S(2)}, u32[]{:S(2)}) collective-permute-start(bf16[512,768]{1,0:T(8,128)(2,1)} %get-tuple-element.55), channel_id=1, source_target_pairs={{0,1},{1,0},{2,3},{3,2},{4,5},{5,4},{6,7},{7,6},{8,9},{9,8},{10,11... | collective-permute-start | bytes 2359304 | tf_op jit(solution)/shard_map/ppermute | solution.py:460
  196.4 118.6 %collective-permute-start.26 = (bf16[512,768]{1,0:T(8,128)(2,1)}, bf16[512,768]{1,0:T(8,128)(2,1)}, u32[]{:S(2)}, u32[]{:S(2)}) collective-permute-start(bf16[512,768]{1,0:T(8,128)(2,1)} %get-tuple-element.48.o_ref.ao), channel_id=1, source_target_pairs={{0,1},{1,0},{2,3},{3,2},{4,5},{5,4},{6,7},{7,6},{8,9},{9,8},{10,11... | collective-permute-start | bytes 2359304 | tf_op jit(solution)/shard_map/ppermute | solution.py:460
  253.1 18.9 %collective-permute-start.8 = (bf16[512,768]{1,0:T(8,128)(2,1)}, bf16[512,768]{1,0:T(8,128)(2,1)}, u32[]{:S(2)}, u32[]{:S(2)}) collective-permute-start(bf16[512,768]{1,0:T(8,128)(2,1)} %get-tuple-element.65), channel_id=1, source_target_pairs={{0,1},{1,0},{2,3},{3,2},{4,5},{5,4},{6,7},{7,6},{8,9},{9,8},{10,11... | collective-permute-start | bytes 2359304 | tf_op jit(solution)/shard_map/ppermute | solution.py:460
  253.2 21.0 %collective-permute-start.7 = (bf16[512,768]{1,0:T(8,128)(2,1)}, bf16[512,768]{1,0:T(8,128)(2,1)}, u32[]{:S(2)}, u32[]{:S(2)}) collective-permute-start(bf16[512,768]{1,0:T(8,128)(2,1)} %get-tuple-element.63), channel_id=1, source_target_pairs={{0,1},{1,0},{2,3},{3,2},{4,5},{5,4},{6,7},{7,6},{8,9},{9,8},{10,11... | collective-permute-start | bytes 2359304 | tf_op jit(solution)/shard_map/ppermute | solution.py:460
  272.0 18.4 %collective-permute-start.44 = (bf16[512,768]{1,0:T(8,128)(2,1)}, bf16[512,768]{1,0:T(8,128)(2,1)}, u32[]{:S(2)}, u32[]{:S(2)}) collective-permute-start(bf16[512,768]{1,0:T(8,128)(2,1)} %add_convert_fusion.7.normed_ref.ao), channel_id=1, source_target_pairs={{0,1},{1,0},{2,3},{3,2},{4,5},{5,4},{6,7},{7,6},{8,9},{9,8},{10,11... | collective-permute-start | bytes 2359304 | tf_op jit(solution)/shard_map/ppermute | solution.py:460
  274.2 16.7 %collective-permute-start.45 = (bf16[512,1536]{1,0:T(8,128)(2,1)}, bf16[512,1536]{1,0:T(8,128)(2,1)}, u32[]{:S(2)}, u32[]{:S(2)}) collective-permute-start(bf16[512,1536]{1,0:T(8,128)(2,1)} %dynamic-slice_bitcast_fusion), channel_id=1, source_target_pairs={{0,1},{1,0},{2,3},{3,2},{4,5},{5,4},{6,7},{7,6},{8,9},{9,8},{10,11... | collective-permute-start | bytes 4718600 | tf_op jit(solution)/shard_map/ppermute | solution.py:460
  290.5 24.6 %collective-permute-start.25 = (bf16[512,1152]{1,0:T(8,128)(2,1)}, bf16[512,1152]{1,0:T(8,128)(2,1)}, u32[]{:S(2)}, u32[]{:S(2)}) collective-permute-start(bf16[512,1152]{1,0:T(8,128)(2,1)} %constant_dynamic-slice_fusion.7), channel_id=1, source_target_pairs={{0,1},{1,0},{2,3},{3,2},{4,5},{5,4},{6,7},{7,6},{8,9},{9,8},{10,11... | collective-permute-start | bytes 3538952 | tf_op jit(solution)/shard_map/ppermute | solution.py:460
  291.0 8.2 %collective-permute-start.10 = (f32[16,8,24]{2,1,0:T(8,128)S(1)}, f32[16,8,24]{2,1,0:T(8,128)S(1)}, u32[]{:S(2)}, u32[]{:S(2)}) collective-permute-start(f32[16,8,24]{2,1,0:T(8,128)S(1)} %dynamic-slice_bitcast_fusion.14), channel_id=1, source_target_pairs={{0,1},{1,0},{2,3},{3,2},{4,5},{5,4},{6,7},{7,6},{8,9},{9,8},{10,11... | collective-permute-start | bytes 36872 | tf_op jit(solution)/shard_map/ppermute | solution.py:460
  303.0 4.0 collective-permute-start.11
  307.0 3.7 collective-permute-start.12
  310.7 1.7 collective-permute-start.27
  310.7 3.7 collective-permute-start.13
  312.4 11.2 %collective-permute-start.35 = (bf16[512,768]{1,0:T(8,128)(2,1)}, bf16[512,768]{1,0:T(8,128)(2,1)S(1)}, u32[]{:S(2)}, u32[]{:S(2)}) collective-permute-start(bf16[512,768]{1,0:T(8,128)(2,1)} %add_convert_fusion.9.normed_ref.ao), channel_id=1, source_target_pairs={{0,1},{1,0},{2,3},{3,2},{4,5},{5,4},{6,7},{7,6},{8,9},{9,8},{10,11... | collective-permute-start | bytes 2359304 | tf_op jit(solution)/shard_map/ppermute | solution.py:460
  314.4 23.2 %collective-permute-start.36 = (bf16[512,1536]{1,0:T(8,128)(2,1)}, bf16[512,1536]{1,0:T(8,128)(2,1)}, u32[]{:S(2)}, u32[]{:S(2)}) collective-permute-start(bf16[512,1536]{1,0:T(8,128)(2,1)} %dynamic-slice_bitcast_fusion.1), channel_id=1, source_target_pairs={{0,1},{1,0},{2,3},{3,2},{4,5},{5,4},{6,7},{7,6},{8,9},{9,8},{10,11... | collective-permute-start | bytes 4718600 | tf_op jit(solution)/shard_map/ppermute | solution.py:460
  315.0 56.2 %collective-permute-start.42 = (bf16[512,3072]{1,0:T(8,128)(2,1)}, bf16[512,3072]{1,0:T(8,128)(2,1)}, u32[]{:S(2)}, u32[]{:S(2)}) collective-permute-start(bf16[512,3072]{1,0:T(8,128)(2,1)} %get-tuple-element.76.ao), channel_id=1, source_target_pairs={{0,1},{1,0},{2,3},{3,2},{4,5},{5,4},{6,7},{7,6},{8,9},{9,8},{10,11... | collective-permute-start | bytes 9437192 | tf_op jit(solution)/shard_map/ppermute | solution.py:460
  315.1 10.5 %collective-permute-start.14 = (f32[1,8,24]{2,1,0:T(8,128)S(1)}, f32[1,8,24]{2,1,0:T(8,128)S(1)}, u32[]{:S(2)}, u32[]{:S(2)}) collective-permute-start(f32[1,8,24]{2,1,0:T(8,128)S(1)} %slice_add_fusion.3), channel_id=1, source_target_pairs={{0,16},{1,17},{2,18},{3,19},{4,20},{5,21},{6,22},{7,23},{8,24},{9,... | collective-permute-start | bytes 2312 | tf_op jit(solution)/shard_map/ppermute | solution.py:498
  323.7 11.4 %collective-permute-start.9 = (bf16[256,768]{1,0:T(8,128)(2,1)S(1)}, bf16[256,768]{1,0:T(8,128)(2,1)S(1)}, u32[]{:S(2)}, u32[]{:S(2)}) collective-permute-start(bf16[256,768]{1,0:T(8,128)(2,1)S(1)} %get-tuple-element.118), channel_id=1, source_target_pairs={{0,3},{1,2},{2,1},{3,0},{4,7},{5,6},{6,5},{7,4},{8,11},{9,10},{10,... | collective-permute-start | bytes 1179656 | tf_op jit(solution)/shard_map/ppermute | solution.py:463
  325.6 20.7 %collective-permute-start.28 = (bf16[8,48,1536]{2,1,0:T(8,128)(2,1)}, bf16[8,48,1536]{2,1,0:T(8,128)(2,1)S(1)}, u32[]{:S(2)}, u32[]{:S(2)}) collective-permute-start(bf16[8,48,1536]{2,1,0:T(8,128)(2,1)} %get-tuple-element.69), channel_id=1, source_target_pairs={{0,4},{1,3},{2,6},{3,1},{4,0},{5,7},{6,2},{7,5},{8,12},{9,11},{10,... | collective-permute-start | bytes 3538952 | tf_op jit(solution)/shard_map/ppermute | solution.py:498
  335.1 10.7 %collective-permute-start.15 = (bf16[512,768]{1,0:T(8,128)(2,1)S(1)}, bf16[512,768]{1,0:T(8,128)(2,1)S(1)}, u32[]{:S(2)}, u32[]{:S(2)}) collective-permute-start(bf16[512,768]{1,0:T(8,128)(2,1)S(1)} %copy-done.43), channel_id=1, source_target_pairs={{0,1},{1,0},{2,3},{3,2},{4,5},{5,4},{6,7},{7,6},{8,9},{9,8},{10,11... | collective-permute-start | bytes 2359304 | tf_op jit(solution)/shard_map/ppermute | solution.py:460
  337.7 22.5 %collective-permute-start.16 = (bf16[512,1152]{1,0:T(8,128)(2,1)S(1)}, bf16[512,1152]{1,0:T(8,128)(2,1)}, u32[]{:S(2)}, u32[]{:S(2)}) collective-permute-start(bf16[512,1152]{1,0:T(8,128)(2,1)S(1)} %constant_dynamic-slice_fusion.9), channel_id=1, source_target_pairs={{0,1},{1,0},{2,3},{3,2},{4,5},{5,4},{6,7},{7,6},{8,9},{9,8},{10,11... | collective-permute-start | bytes 3538952 | tf_op jit(solution)/shard_map/ppermute | solution.py:460
  345.8 14.2 %collective-permute-start.17 = (bf16[512,768]{1,0:T(8,128)(2,1)S(1)}, bf16[512,768]{1,0:T(8,128)(2,1)}, u32[]{:S(2)}, u32[]{:S(2)}) collective-permute-start(bf16[512,768]{1,0:T(8,128)(2,1)S(1)} %copy-done.103), channel_id=1, source_target_pairs={{0,1},{1,0},{2,3},{3,2},{4,5},{5,4},{6,7},{7,6},{8,9},{9,8},{10,11... | collective-permute-start | bytes 2359304 | tf_op jit(solution)/shard_map/ppermute | solution.py:460
  346.3 2.8 collective-permute-start.34
  349.1 10.9 %collective-permute-start.18 = (bf16[512,384]{1,0:T(8,128)(2,1)S(1)}, bf16[512,384]{1,0:T(8,128)(2,1)S(1)}, u32[]{:S(2)}, u32[]{:S(2)}) collective-permute-start(bf16[512,384]{1,0:T(8,128)(2,1)S(1)} %copy-done.53), channel_id=1, source_target_pairs={{0,1},{1,0},{2,3},{3,2},{4,5},{5,4},{6,7},{7,6},{8,9},{9,8},{10,11... | collective-permute-start | bytes 1179656 | tf_op jit(solution)/shard_map/ppermute | solution.py:460
  349.5 21.2 %collective-permute-start.29 = (bf16[4,48,1536]{2,1,0:T(8,128)(2,1)S(1)}, bf16[4,48,1536]{2,1,0:T(8,128)(2,1)S(1)}, u32[]{:S(2)}, u32[]{:S(2)}) collective-permute-start(bf16[4,48,1536]{2,1,0:T(8,128)(2,1)S(1)} %add_convert_fusion.12), channel_id=1, source_target_pairs={{0,2},{1,5},{2,0},{3,7},{4,6},{5,1},{6,4},{7,3},{8,10},{9,13},{10,... | collective-permute-start | bytes 1769480 | tf_op jit(solution)/shard_map/ppermute | solution.py:498
  360.0 11.2 %collective-permute-start.43 = (bf16[512,384]{1,0:T(8,128)(2,1)S(1)}, bf16[512,384]{1,0:T(8,128)(2,1)S(1)}, u32[]{:S(2)}, u32[]{:S(2)}) collective-permute-start(bf16[512,384]{1,0:T(8,128)(2,1)S(1)} %copy-done.52), channel_id=1, source_target_pairs={{0,1},{1,0},{2,3},{3,2},{4,5},{5,4},{6,7},{7,6},{8,9},{9,8},{10,11... | collective-permute-start | bytes 1179656 | tf_op jit(solution)/shard_map/ppermute | solution.py:460
  360.1 71.0 %collective-permute-start.37 = (bf16[8,192,768]{2,1,0:T(8,128)(2,1)}, bf16[8,192,768]{2,1,0:T(8,128)(2,1)S(1)}, u32[]{:S(2)}, u32[]{:S(2)}) collective-permute-start(bf16[8,192,768]{2,1,0:T(8,128)(2,1)} %get-tuple-element.75), channel_id=1, source_target_pairs={{0,4},{1,3},{2,6},{3,1},{4,0},{5,7},{6,2},{7,5},{8,12},{9,11},{10,... | collective-permute-start | bytes 7077896 | tf_op jit(solution)/shard_map/ppermute | solution.py:498
  369.3 32.5 %collective-permute-start.19 = (bf16[8,48,1536]{2,1,0:T(8,128)(2,1)}, bf16[8,48,1536]{2,1,0:T(8,128)(2,1)S(1)}, u32[]{:S(2)}, u32[]{:S(2)}) collective-permute-start(bf16[8,48,1536]{2,1,0:T(8,128)(2,1)} %get-tuple-element.67), channel_id=1, source_target_pairs={{0,4},{1,3},{2,6},{3,1},{4,0},{5,7},{6,2},{7,5},{8,12},{9,11},{10,... | collective-permute-start | bytes 3538952 | tf_op jit(solution)/shard_map/ppermute | solution.py:498
  370.8 10.8 %collective-permute-start.30 = (bf16[2,48,1536]{2,1,0:T(8,128)(2,1)S(1)}, bf16[2,48,1536]{2,1,0:T(8,128)(2,1)S(1)}, u32[]{:S(2)}, u32[]{:S(2)}) collective-permute-start(bf16[2,48,1536]{2,1,0:T(8,128)(2,1)S(1)} %add_convert_fusion.16), channel_id=1, source_target_pairs={{0,8},{1,9},{2,10},{3,11},{4,12},{5,13},{6,14},{7,15},{8,0},{9,1},... | collective-permute-start | bytes 884744 | tf_op jit(solution)/shard_map/ppermute | solution.py:498
  380.9 57.3 %collective-permute-start.46 = (bf16[8,192,768]{2,1,0:T(8,128)(2,1)}, bf16[8,192,768]{2,1,0:T(8,128)(2,1)S(1)}, u32[]{:S(2)}, u32[]{:S(2)}) collective-permute-start(bf16[8,192,768]{2,1,0:T(8,128)(2,1)} %get-tuple-element.81), channel_id=1, source_target_pairs={{0,4},{1,3},{2,6},{3,1},{4,0},{5,7},{6,2},{7,5},{8,12},{9,11},{10,... | collective-permute-start | bytes 7077896 | tf_op jit(solution)/shard_map/ppermute | solution.py:498
  382.7 19.9 %collective-permute-start.31 = (bf16[1,48,1536]{2,1,0:T(8,128)(2,1)S(1)}, bf16[1,48,1536]{2,1,0:T(8,128)(2,1)S(1)}, u32[]{:S(2)}, u32[]{:S(2)}) collective-permute-start(bf16[1,48,1536]{2,1,0:T(8,128)(2,1)S(1)} %add_convert_fusion.18), channel_id=1, source_target_pairs={{0,16},{1,17},{2,18},{3,19},{4,20},{5,21},{6,22},{7,23},{8,24},{9,... | collective-permute-start | bytes 442376 | tf_op jit(solution)/shard_map/ppermute | solution.py:498
  402.0 16.3 %collective-permute-start.20 = (bf16[4,48,1536]{2,1,0:T(8,128)(2,1)S(1)}, bf16[4,48,1536]{2,1,0:T(8,128)(2,1)S(1)}, u32[]{:S(2)}, u32[]{:S(2)}) collective-permute-start(bf16[4,48,1536]{2,1,0:T(8,128)(2,1)S(1)} %add_convert_fusion.13), channel_id=1, source_target_pairs={{0,2},{1,5},{2,0},{3,7},{4,6},{5,1},{6,4},{7,3},{8,10},{9,13},{10,... | collective-permute-start | bytes 1769480 | tf_op jit(solution)/shard_map/ppermute | solution.py:498
  419.4 7.7 %collective-permute-start.21 = (bf16[2,48,1536]{2,1,0:T(8,128)(2,1)S(1)}, bf16[2,48,1536]{2,1,0:T(8,128)(2,1)S(1)}, u32[]{:S(2)}, u32[]{:S(2)}) collective-permute-start(bf16[2,48,1536]{2,1,0:T(8,128)(2,1)S(1)} %add_convert_fusion.17), channel_id=1, source_target_pairs={{0,8},{1,9},{2,10},{3,11},{4,12},{5,13},{6,14},{7,15},{8,0},{9,1},... | collective-permute-start | bytes 884744 | tf_op jit(solution)/shard_map/ppermute | solution.py:498
  428.1 7.7 %collective-permute-start.22 = (bf16[1,48,1536]{2,1,0:T(8,128)(2,1)S(1)}, bf16[1,48,1536]{2,1,0:T(8,128)(2,1)S(1)}, u32[]{:S(2)}, u32[]{:S(2)}) collective-permute-start(bf16[1,48,1536]{2,1,0:T(8,128)(2,1)S(1)} %add_convert_fusion.19), channel_id=1, source_target_pairs={{0,16},{1,17},{2,18},{3,19},{4,20},{5,21},{6,22},{7,23},{8,24},{9,... | collective-permute-start | bytes 442376 | tf_op jit(solution)/shard_map/ppermute | solution.py:498
  431.3 16.3 %collective-permute-start.38 = (bf16[4,192,768]{2,1,0:T(8,128)(2,1)S(1)}, bf16[4,192,768]{2,1,0:T(8,128)(2,1)S(1)}, u32[]{:S(2)}, u32[]{:S(2)}) collective-permute-start(bf16[4,192,768]{2,1,0:T(8,128)(2,1)S(1)} %add_convert_fusion.1), channel_id=1, source_target_pairs={{0,2},{1,5},{2,0},{3,7},{4,6},{5,1},{6,4},{7,3},{8,10},{9,13},{10,... | collective-permute-start | bytes 3538952 | tf_op jit(solution)/shard_map/ppermute | solution.py:498
  438.6 26.3 %collective-permute-start.47 = (bf16[4,192,768]{2,1,0:T(8,128)(2,1)S(1)}, bf16[4,192,768]{2,1,0:T(8,128)(2,1)S(1)}, u32[]{:S(2)}, u32[]{:S(2)}) collective-permute-start(bf16[4,192,768]{2,1,0:T(8,128)(2,1)S(1)} %add_convert_fusion), channel_id=1, source_target_pairs={{0,2},{1,5},{2,0},{3,7},{4,6},{5,1},{6,4},{7,3},{8,10},{9,13},{10,... | collective-permute-start | bytes 3538952 | tf_op jit(solution)/shard_map/ppermute | solution.py:498
  447.8 13.9 %collective-permute-start.39 = (bf16[2,192,768]{2,1,0:T(8,128)(2,1)S(1)}, bf16[2,192,768]{2,1,0:T(8,128)(2,1)S(1)}, u32[]{:S(2)}, u32[]{:S(2)}) collective-permute-start(bf16[2,192,768]{2,1,0:T(8,128)(2,1)S(1)} %add_convert_fusion.11), channel_id=1, source_target_pairs={{0,8},{1,9},{2,10},{3,11},{4,12},{5,13},{6,14},{7,15},{8,0},{9,1},... | collective-permute-start | bytes 1769480 | tf_op jit(solution)/shard_map/ppermute | solution.py:498
  461.9 16.2 %collective-permute-start.40 = (bf16[1,192,768]{2,1,0:T(8,128)(2,1)S(1)}, bf16[1,192,768]{2,1,0:T(8,128)(2,1)S(1)}, u32[]{:S(2)}, u32[]{:S(2)}) collective-permute-start(bf16[1,192,768]{2,1,0:T(8,128)(2,1)S(1)} %add_convert_fusion.15), channel_id=1, source_target_pairs={{0,16},{1,17},{2,18},{3,19},{4,20},{5,21},{6,22},{7,23},{8,24},{9,... | collective-permute-start | bytes 884744 | tf_op jit(solution)/shard_map/ppermute | solution.py:498
  466.1 21.3 %collective-permute-start.48 = (bf16[2,192,768]{2,1,0:T(8,128)(2,1)}, bf16[2,192,768]{2,1,0:T(8,128)(2,1)}, u32[]{:S(2)}, u32[]{:S(2)}) collective-permute-start(bf16[2,192,768]{2,1,0:T(8,128)(2,1)} %add_convert_fusion.10), channel_id=1, source_target_pairs={{0,8},{1,9},{2,10},{3,11},{4,12},{5,13},{6,14},{7,15},{8,0},{9,1},... | collective-permute-start | bytes 1769480 | tf_op jit(solution)/shard_map/ppermute | solution.py:498
  479.7 9.6 %collective-permute-start.41 = (f32[96,768]{1,0:T(8,128)}, f32[96,768]{1,0:T(8,128)}, u32[]{:S(2)}, u32[]{:S(2)}) collective-permute-start(f32[96,768]{1,0:T(8,128)} %pad_maximum_fusion.5), channel_id=1, source_target_pairs={{0,1},{1,0},{2,3},{3,2},{4,5},{5,4},{6,7},{7,6},{8,9},{9,8},{10,11... | collective-permute-start | bytes 884744 | tf_op jit(solution)/shard_map/ppermute | solution.py:460
  489.3 13.9 %collective-permute-start.49 = (bf16[1,192,768]{2,1,0:T(8,128)(2,1)}, bf16[1,192,768]{2,1,0:T(8,128)(2,1)S(1)}, u32[]{:S(2)}, u32[]{:S(2)}) collective-permute-start(bf16[1,192,768]{2,1,0:T(8,128)(2,1)} %add_convert_fusion.14), channel_id=1, source_target_pairs={{0,16},{1,17},{2,18},{3,19},{4,20},{5,21},{6,22},{7,23},{8,24},{9,... | collective-permute-start | bytes 884744 | tf_op jit(solution)/shard_map/ppermute | solution.py:498
  (115 other events, 1052.5 us)
